TPU v7x, 512 devices: a whole 4x4x16 slice. The times are simulated.
512 devices in a mesh: dp: 4 (over y), node: 16 (over z), local: 8 (over x, core).
Axes of the slice: x: 4, y: 4, z: 16, core: 2. Of those that a mesh axis runs over, the one named last changes fastest.
Arguments:
- tokens: bfloat16 [32768, 1024], P(('dp', 'node', 'local')), may hold values from -6 to 6
- upstream: bfloat16 [32768, 1024], P(('dp', 'node', 'local')), may hold values from -1.1953125 to 1.1953125
- expert_ids: int32 [32768, 4], P(('dp', 'node', 'local')), may hold values from 0 to 63, as said below
- gate_weights: bfloat16 [32768, 4], P(('dp', 'node', 'local')), may hold values from 0.099609375 to 1
- w_gate: bfloat16 [128, 352, 1024], P(('node', 'local')), may hold values from -0.1875 to 0.1875
- w_up: bfloat16 [128, 352, 1024], P(('node', 'local')), may hold values from -0.1875 to 0.1875
- w_down: bfloat16 [128, 352, 1024], P(('node', 'local')), may hold values from -0.21875 to 0.21875
Outputs:
- token_grads: bfloat16 [32768, 1024], P(('dp', 'node', 'local'))
- gate_grads: bfloat16 [128, 352, 1024], P(('node', 'local'), None, 'dp')
- up_grads: bfloat16 [128, 352, 1024], P(('node', 'local'), None, 'dp')
- down_grads: bfloat16 [128, 352, 1024], P(('node', 'local'), None, 'dp')
Inputs may be any that keep to these rules, and one draw needn't show every extreme that they name: `expert_ids`: each row names 4 distinct experts, lying on exactly 3 distinct nodes, expert e lying on node e // 4. Of one device's 64 rows, exactly 12 name some expert on any given node, and at most 5 name any one expert; in every draw some experts are named by exactly 5 rows of every device.
All inputs are finite; a program needn't handle non-finite values.
Results may differ from a plain program's by a relative error of at most 0.013.
Values may be sent and summed in bfloat16 or wider, within the bound.
No kernel may reach another device: no remote copies, remote signals or barrier semaphores. Data moves between devices by JAX's collectives and lax.ppermute only.
A program may use at most 64 MiB of HBM per device.

v0:
```python
import jax
import jax.numpy as jnp
from jax import lax
from jax.sharding import PartitionSpec as P

contract_last = (((1,), (1,)), ((), ()))
contract_first = (((0,), (0,)), ((), ()))


def expert_backward(x_rows, cot_rows, gate_half, up_half, down_half):
    gate_logit = lax.dot_general(
        x_rows, gate_half, contract_last, preferred_element_type=jnp.float32
    )
    up_value = lax.dot_general(x_rows, up_half, contract_last, preferred_element_type=jnp.float32)
    gate_sigmoid = jax.nn.sigmoid(gate_logit)
    activation = gate_logit * gate_sigmoid
    hidden = (activation * up_value).astype(jnp.bfloat16)
    back_hidden = lax.dot_general(
        cot_rows, down_half, contract_last, preferred_element_type=jnp.float32
    )
    back_up = (back_hidden * activation).astype(jnp.bfloat16)
    back_gate = (
        back_hidden * up_value * gate_sigmoid * (1.0 + gate_logit * (1.0 - gate_sigmoid))
    ).astype(jnp.bfloat16)
    partial_value = jnp.dot(back_gate, gate_half, preferred_element_type=jnp.float32) + jnp.dot(
        back_up, up_half, preferred_element_type=jnp.float32
    )
    grad_gate = lax.dot_general(
        back_gate, x_rows, contract_first, preferred_element_type=jnp.float32
    )
    grad_up = lax.dot_general(back_up, x_rows, contract_first, preferred_element_type=jnp.float32)
    grad_down = lax.dot_general(
        hidden, cot_rows, contract_first, preferred_element_type=jnp.float32
    )
    return (partial_value.astype(jnp.bfloat16), grad_gate, grad_up, grad_down)


def routing_slots(expert_ids, experts):
    row_count, top = expert_ids.shape
    flat_ids = expert_ids.reshape(row_count * top)
    onehot = (flat_ids[:, None] == jnp.arange(experts, dtype=jnp.int32)[None, :]).astype(jnp.int32)
    earlier = jnp.cumsum(onehot, axis=0) - onehot
    slots = jnp.sum(earlier * onehot, axis=1)
    owners = jnp.arange(row_count * top, dtype=jnp.int32) // top
    return (flat_ids, slots, owners)


def both_halves(rows, per_node):
    shape = rows.shape
    doubled = jnp.broadcast_to(rows[:, None], (shape[0], 2) + shape[1:])
    return doubled.reshape((2 * per_node,) + shape[1:])


def node_total(gathered, node_choice):
    row_count, top, width = gathered.shape
    total = jnp.zeros((row_count, width), jnp.float32)
    for column in range(top):
        same_node = node_choice == node_choice[:, column : column + 1]
        node_piece = jnp.sum(jnp.where(same_node[:, :, None], gathered, 0.0), axis=1)
        if column == 0:
            leading = jnp.ones((row_count,), bool)
        else:
            leading = jnp.all(
                node_choice[:, :column] != node_choice[:, column : column + 1], axis=1
            )
        stored = lax.optimization_barrier(node_piece.astype(jnp.bfloat16)).astype(jnp.float32)
        total = total + jnp.where(leading[:, None], stored, 0.0)
    return total


def on_device(tokens, upstream, expert_ids, gate_weights, w_gate, w_up, w_down):
    row_count, width = tokens.shape
    top = expert_ids.shape[1]
    node_count = lax.axis_size("node")
    local_count = lax.axis_size("local")
    per_node = local_count // 2
    experts = node_count * per_node
    node_limit = min(3, node_count - 1)
    share = row_count // experts
    capacity = (node_limit + min(top - node_limit, 1) * (1 + min(max(per_node - 2, 0), 1))) * share
    gate_half = w_gate[0]
    up_half = w_up[0]
    down_half = w_down[0]
    flat_ids, slots, owners = routing_slots(expert_ids, experts)
    flat_gates = gate_weights.reshape(row_count * top)
    zero_row = jnp.zeros((1, width), jnp.bfloat16)
    tokens_pad = jnp.concatenate([tokens, zero_row], 0)
    upstream_pad = jnp.concatenate([upstream, zero_row], 0)
    position = flat_ids * capacity + slots
    source_row = jnp.full((experts * capacity,), row_count, jnp.int32).at[position].set(owners)
    gate_rows = (
        jnp.zeros((experts * capacity,), jnp.float32)
        .at[position]
        .set(flat_gates.astype(jnp.float32))
    )
    x_rows = tokens_pad[source_row].reshape(experts, capacity, width)
    cot_rows = (
        (gate_rows[:, None] * upstream_pad[source_row].astype(jnp.float32))
        .astype(jnp.bfloat16)
        .reshape(experts, capacity, width)
    )
    x_send = both_halves(x_rows, experts)
    cot_send = both_halves(cot_rows, experts)
    x_got, cot_got = (
        lax.all_to_all(x_send, ("node", "local"), split_axis=0, concat_axis=0, tiled=True),
        lax.all_to_all(cot_send, ("node", "local"), split_axis=0, concat_axis=0, tiled=True),
    )
    partial_value, grad_gate, grad_up, grad_down = expert_backward(
        x_got.reshape(-1, width), cot_got.reshape(-1, width), gate_half, up_half, down_half
    )
    pieces = partial_value.reshape(2 * experts, capacity, width)
    returned = lax.all_to_all(pieces, ("node", "local"), split_axis=0, concat_axis=0, tiled=True)
    pair_sum = jnp.sum(
        returned.reshape(experts, 2, capacity, width).astype(jnp.float32), axis=1
    ).reshape(experts * capacity, width)
    gathered = pair_sum[position].reshape(row_count, top, width)
    total = node_total(gathered, expert_ids // per_node)
    summed = (
        lax.psum_scatter(
            grad_gate.astype(jnp.bfloat16), "dp", scatter_dimension=1, tiled=True
        ).astype(jnp.float32),
        lax.psum_scatter(
            grad_up.astype(jnp.bfloat16), "dp", scatter_dimension=1, tiled=True
        ).astype(jnp.float32),
        lax.psum_scatter(
            grad_down.astype(jnp.bfloat16), "dp", scatter_dimension=1, tiled=True
        ).astype(jnp.float32),
    )
    return (
        total.astype(jnp.bfloat16),
        summed[0].astype(jnp.bfloat16)[None],
        summed[1].astype(jnp.bfloat16)[None],
        summed[2].astype(jnp.bfloat16)[None],
    )


def solution(mesh):
    return jax.shard_map(
        on_device,
        mesh=mesh,
        in_specs=(
            P(("dp", "node", "local"), None),
            P(("dp", "node", "local"), None),
            P(("dp", "node", "local"), None),
            P(("dp", "node", "local"), None),
            P(("node", "local"), None, None),
            P(("node", "local"), None, None),
            P(("node", "local"), None, None),
        ),
        out_specs=(
            P(("dp", "node", "local"), None),
            P(("node", "local"), None, "dp"),
            P(("node", "local"), None, "dp"),
            P(("node", "local"), None, "dp"),
        ),
        check_vma=False,
    )
```

profile of v0, /device:TPU:24, one launch (start us, length us, event | category | flops | bytes accessed | tf_op | source)
XLA Modules:
  0.0 375.8 jit_solution(8610314077641069422)
XLA Ops:
  7.9 0.8 copy.17
  10.1 1.4 scatter_custom_fusion.1
  11.5 0.9 concatenate.7
  12.5 2.1 gather_fusion.1
  14.8 1.6 broadcast_in_dim.110
  16.5 19.9 %all-to-all-start.1 = ((bf16[128,5,1024]{2,1,0:T(8,128)(2,1)}), bf16[128,5,1024]{2,1,0:T(8,128)(2,1)S(1)}, u32[]{:S(2)}, u32[]{:S(2)}) async-start(bf16[128,5,1024]{2,1,0:T(8,128)(2,1)} %bitcast.66), calls=%async_computation.1 | async-start | bytes 4194304 | tf_op jit(solution)/shard_map/all_to_all | solution.py:105
  36.6 1.4 scatter_custom_fusion
  38.2 2.6 gather_fusion
  40.8 2.4 reshape.116
  43.2 2.7 multiply_convert_fusion
  46.0 88.6 %all-to-all-done.1 = bf16[128,5,1024]{2,1,0:T(8,128)(2,1)S(1)} async-done(((bf16[128,5,1024]{2,1,0:T(8,128)(2,1)}), bf16[128,5,1024]{2,1,0:T(8,128)(2,1)S(1)}, u32[]{:S(2)}, u32[]{:S(2)}) %all-to-all-start.1) | async-done | bytes 1310752 | tf_op jit(solution)/shard_map/all_to_all | solution.py:105
  134.6 2.9 broadcast_in_dim.108
  137.5 9.4 %all-to-all-start = ((bf16[128,5,1024]{2,1,0:T(8,128)(2,1)}), bf16[128,5,1024]{2,1,0:T(8,128)(2,1)}, u32[]{:S(2)}, u32[]{:S(2)}) async-start(bf16[128,5,1024]{2,1,0:T(8,128)(2,1)} %bitcast.67), calls=%async_computation | async-start | bytes 4194304 | tf_op jit(solution)/shard_map/all_to_all | solution.py:106
  146.9 1.4 reshape.111
  148.3 3.2 fusion.3
  151.5 1.7 fusion.6
  153.2 91.3 %all-to-all-done = bf16[128,5,1024]{2,1,0:T(8,128)(2,1)} async-done(((bf16[128,5,1024]{2,1,0:T(8,128)(2,1)}), bf16[128,5,1024]{2,1,0:T(8,128)(2,1)}, u32[]{:S(2)}, u32[]{:S(2)}) %all-to-all-start) | async-done | bytes 1310752 | tf_op jit(solution)/shard_map/all_to_all | solution.py:106
  244.5 2.6 reshape.109
  247.2 3.0 multiply_convert_fusion.2
  250.2 0.9 fusion.1
  251.1 0.9 add_convert_fusion
  252.0 1.6 reshape.112
  253.6 8.7 %all-to-all-start.2 = ((bf16[128,5,1024]{2,1,0:T(8,128)(2,1)}), bf16[128,5,1024]{2,1,0:T(8,128)(2,1)S(1)}, u32[]{:S(2)}, u32[]{:S(2)}) async-start(bf16[128,5,1024]{2,1,0:T(8,128)(2,1)} %reshape.112), calls=%async_computation.2 | async-start | bytes 4194304 | tf_op jit(solution)/shard_map/all_to_all | solution.py:112
  262.4 3.5 convolution_convert_fusion
  265.9 3.1 convolution_convert_fusion.2
  269.1 2.9 convolution_convert_fusion.1
  272.6 87.9 %all-to-all-done.2 = bf16[128,5,1024]{2,1,0:T(8,128)(2,1)S(1)} async-done(((bf16[128,5,1024]{2,1,0:T(8,128)(2,1)}), bf16[128,5,1024]{2,1,0:T(8,128)(2,1)S(1)}, u32[]{:S(2)}, u32[]{:S(2)}) %all-to-all-start.2) | async-done | bytes 1310752 | tf_op jit(solution)/shard_map/all_to_all | solution.py:112
  360.6 1.9 convert_reduce_fusion
  362.4 1.6 reshape.113
  364.1 1.1 gather_fusion.2
  365.5 3.0 select_reduce_fusion.3
  368.4 0.9 add_convert_fusion.1
  (54 shorter events, 3.8 us)
Async XLA Ops:
  7.2 141.2 %copy-start = (bf16[1,352,1024]{2,1,0:T(8,128)(2,1)S(1)}, bf16[1,352,1024]{2,1,0:T(8,128)(2,1)}, u32[]{:S(2)}) copy-start(bf16[1,352,1024]{2,1,0:T(8,128)(2,1)} %param.11) | copy-start | bytes 2162692
  16.5 19.9 %copy-start.6 = (bf16[64,4]{0,1:T(4,128)(2,1)S(1)}, bf16[64,4]{0,1:T(4,128)(2,1)}, u32[]{:S(2)}) copy-start(bf16[64,4]{0,1:T(4,128)(2,1)} %param.10) | copy-start | bytes 1540
  16.5 21.7 %copy-start.5 = (bf16[64,1024]{1,0:T(8,128)(2,1)S(1)}, bf16[64,1024]{1,0:T(8,128)(2,1)}, u32[]{:S(2)}) copy-start(bf16[64,1024]{1,0:T(8,128)(2,1)} %param.8) | copy-start | bytes 393220
  16.5 118.1 %all-to-all-start.1 = ((bf16[128,5,1024]{2,1,0:T(8,128)(2,1)}), bf16[128,5,1024]{2,1,0:T(8,128)(2,1)S(1)}, u32[]{:S(2)}, u32[]{:S(2)}) async-start(bf16[128,5,1024]{2,1,0:T(8,128)(2,1)} %bitcast.66), calls=%async_computation.1 | async-start | bytes 4194304 | tf_op jit(solution)/shard_map/all_to_all | solution.py:105
  137.5 107.1 %all-to-all-start = ((bf16[128,5,1024]{2,1,0:T(8,128)(2,1)}), bf16[128,5,1024]{2,1,0:T(8,128)(2,1)}, u32[]{:S(2)}, u32[]{:S(2)}) async-start(bf16[128,5,1024]{2,1,0:T(8,128)(2,1)} %bitcast.67), calls=%async_computation | async-start | bytes 4194304 | tf_op jit(solution)/shard_map/all_to_all | solution.py:106
  148.3 3.2 copy-start.1
  148.3 3.2 copy-start.3
  247.1 3.1 copy-start.2
  250.2 0.9 copy-start.4
  253.6 106.9 %all-to-all-start.2 = ((bf16[128,5,1024]{2,1,0:T(8,128)(2,1)}), bf16[128,5,1024]{2,1,0:T(8,128)(2,1)S(1)}, u32[]{:S(2)}, u32[]{:S(2)}) async-start(bf16[128,5,1024]{2,1,0:T(8,128)(2,1)} %reshape.112), calls=%async_computation.2 | async-start | bytes 4194304 | tf_op jit(solution)/shard_map/all_to_all | solution.py:112
  262.3 107.0 %reduce-scatter.8.cloned.1.call-start = ((), (), s32[]{:S(2)}) async-start(), calls=%async_computation.8 | async-start | bytes 901120 | tf_op jit(solution)/shard_map/reduce_scatter | solution.py:125
  265.9 103.4 %reduce-scatter.4.cloned.1.call-start = ((), (), s32[]{:S(2)}) async-start(), calls=%async_computation.6 | async-start | bytes 901120 | tf_op jit(solution)/shard_map/reduce_scatter | solution.py:119
  269.0 100.3 %reduce-scatter.6.cloned.1.call-start = ((), (), s32[]{:S(2)}) async-start(), calls=%async_computation.7 | async-start | bytes 901120 | tf_op jit(solution)/shard_map/reduce_scatter | solution.py:122
Sparse Core Ops, SparseCore 0:
  266.6 28.3 reduce-scatter.7
  298.4 29.6 reduce-scatter.3
  331.6 29.6 reduce-scatter.5
where the time goes:
time: 377 us; the launch traced here: 376 us
  waiting for transfers between devices  268 us (71%)
  starting transfers between devices  38.2 us (10%)
  local copies, waits for them, and re-layouts  26.5 us (7%)
  matrix products  19.2 us (5%)
  between operations  14 us (4%)
  other arithmetic  10.1 us (3%)
    all_to_all x1, waiting for transfers between devices, on_device(): lax.all_to_all(cot_send, ('node', 'local'), split_axis=0, concat_axis=0,...  91.3 us
    all_to_all x1, waiting for transfers between devices, on_device(): lax.all_to_all(x_send, ('node', 'local'), split_axis=0, concat_axis=0, ti...  88.6 us
    all_to_all x1, waiting for transfers between devices, on_device(): lax.all_to_all(pieces, ('node', 'local'), split_axis=0, concat_axis=0, ti...  87.9 us
    all_to_all x1, starting transfers between devices, on_device(): lax.all_to_all(x_send, ('node', 'local'), split_axis=0, concat_axis=0, ti...  19.9 us
    all_to_all x1, starting transfers between devices, on_device(): lax.all_to_all(cot_send, ('node', 'local'), split_axis=0, concat_axis=0,...  9.42 us
    all_to_all x1, starting transfers between devices, on_device(): lax.all_to_all(pieces, ('node', 'local'), split_axis=0, concat_axis=0, ti...  8.71 us
  transfers between devices with their start and end apart: 6, of which 3 were waited for; matrix products, arithmetic and copies ran while one was open for 9% of the time, Pallas kernels for 0%

commit v1 on v0

v1 whole, which is shorter than its diff:
```python
import jax
import jax.numpy as jnp
from jax import lax
from jax.experimental import pallas as pl
from jax.experimental.pallas import tpu as pltpu
from jax.sharding import PartitionSpec as P

WIDTH = 1024
MID = 512
WIDE = 1536
META = 1664
HALF = 352
TOKS = 64
NODES = 16
MSG = 128
CAP = 5
SLOT = 80
SENT = 320
ROWS = 640
F32 = jnp.float32
BF = jnp.bfloat16
SAME_CORE = [[0, 2, 4, 6], [1, 3, 5, 7]]
OTHER_CORE = [(i, i ^ 1) for i in range(8)]


def mm(a, b):
    return jnp.dot(a, b, preferred_element_type=F32)


def mm_first(a, b):
    return lax.dot_general(a, b, (((0,), (0,)), ((), ())), preferred_element_type=F32)


def mm_last(a, b):
    return lax.dot_general(a, b, (((1,), (1,)), ((), ())), preferred_element_type=F32)


def iota(shape, dim):
    return lax.broadcasted_iota(jnp.int32, shape, dim)


def one(cond):
    return jnp.where(cond, 1.0, 0.0).astype(BF)


def route_body(tok_ref, up_ref, ids_ref, gate_ref, xmsg_ref, umsg_ref, sel_ref):
    ids = ids_ref[...]
    gates = gate_ref[...].astype(F32)
    lane_node = iota((TOKS, MSG), 1) >> 3
    lane_expert = iota((TOKS, TOKS), 1)
    named = jnp.zeros((TOKS, MSG), F32)
    weight = jnp.zeros((TOKS, TOKS), F32)
    for k in range(4):
        column = ids[:, k : k + 1]
        named = jnp.where((column >> 2) == lane_node, 1.0, named)
        weight = jnp.where(column == lane_expert, gates[:, k : k + 1], weight)
    named = named.astype(BF)
    weight = weight.astype(BF)
    row, col = iota((TOKS, TOKS), 0), iota((TOKS, TOKS), 1)
    hit = mm_first(named, one(row == col)) > 0.5
    rank = mm_first(named, one(row < col)).astype(jnp.int32)
    place = iota((MSG, TOKS), 0) & 7
    late = hit & (rank == 8 + (place & 3))
    whole = one(hit & (rank == place))
    left = one(late & (place < 4))
    right = one(late & (place >= 4))
    sel_ref[0] = whole
    sel_ref[1] = left
    sel_ref[2] = right
    for src, dst in ((tok_ref, xmsg_ref), (up_ref, umsg_ref)):
        dst[:, :WIDTH] = mm(whole, src[...]).astype(BF)
        dst[:, WIDTH:WIDE] = (mm(left, src[:, :MID]) + mm(right, src[:, MID:])).astype(BF)
    own_node = (iota((MSG, TOKS), 1) >> 2) == (iota((MSG, TOKS), 0) >> 3)
    gate_whole = jnp.where(own_node, mm(whole, weight), 0.0).astype(BF)
    gate_late = jnp.where(own_node, mm(left + right, weight), 0.0).astype(BF)
    fold_row, fold_col = iota((TOKS, MSG), 0) & 3, iota((TOKS, MSG), 1)
    meta = mm(gate_whole, one(fold_col == fold_row)) + mm(gate_late, one(fold_col == fold_row + 8))
    xmsg_ref[:, WIDE:] = meta.astype(BF)


def spread(sel, msg_ref, out_ref):
    low = msg_ref[:, WIDTH:WIDE]
    out_ref[:, :MID] = (mm(sel[:, :MSG], msg_ref[:, :MID]) + mm(sel[:, MSG : 2 * MSG], low)).astype(BF)
    out_ref[:, MID:] = (mm(sel[:, :MSG], msg_ref[:, MID:WIDTH]) + mm(sel[:, 2 * MSG :], low)).astype(BF)


def place_body(msg_ref, out_ref, sel_ref, gated_ref):
    row, col = iota((MSG, MSG), 0), iota((MSG, MSG), 1)
    gates = mm_first(msg_ref[:, WIDE:], one(row == col))
    gate_whole, gate_late = gates[0:8], gates[8:16]
    has_whole, has_late = one(gate_whole > 0.0), one(gate_late > 0.0)
    same = (row >> 3) == (col >> 3)
    rank_whole = mm(has_whole, one(same & (row < col)))
    rank_late = mm(has_whole, one(same)) + mm(has_late, one(same & ((row & 7) < (col & 3))))
    node = (iota((8, MSG), 1) >> 3) * CAP
    lane_place = iota((8, MSG), 1) & 7
    slot_whole = jnp.where(gate_whole > 0.0, node + rank_whole.astype(jnp.int32), -1)
    slot_late = jnp.where(gate_late > 0.0, node + rank_late.astype(jnp.int32), -1)
    slot_left = jnp.where(lane_place < 4, slot_late, -1)
    slot_right = jnp.where(lane_place >= 4, slot_late, -1)
    slots = iota((SLOT, MSG), 0)
    for j in range(4):
        parts = ((slot_whole, gate_whole), (slot_left, gate_late), (slot_right, gate_late))
        for part, (slot, gate) in enumerate(parts):
            match = slots == slot[j : j + 1]
            rows, lanes = pl.ds(j * SLOT, SLOT), pl.ds(part * MSG, MSG)
            sel_ref[rows, lanes] = one(match)
            gated_ref[rows, lanes] = jnp.where(match, gate[j : j + 1], 0.0).astype(BF)
    spread(sel_ref, msg_ref, out_ref)


def cotangent_body(msg_ref, gated_ref, out_ref):
    spread(gated_ref, msg_ref, out_ref)


def forward_body(own_ref, rest_ref, gate_ref, up_ref, act_ref, slope_ref, hidden_ref):
    for source, base in ((own_ref, 0), (rest_ref, SENT)):
        for start in range(0, SENT, 160):
            rows = source[start : start + 160]
            out = pl.ds(base + start, 160)
            gate_logit = mm_last(rows, gate_ref[...])
            up_value = mm_last(rows, up_ref[...])
            sig = jax.nn.sigmoid(gate_logit)
            act = gate_logit * sig
            act_ref[out] = act
            hidden_ref[out] = (act * up_value).astype(BF)
            slope_ref[out] = up_value * sig * (1.0 + gate_logit * (1.0 - sig))


def backward_body(own_ref, rest_ref, down_ref, gate_ref, up_ref, act_ref, slope_ref, piece_own, piece_rest, bg_ref, bu_ref):
    for source, target, base in ((rest_ref, piece_rest, SENT), (own_ref, piece_own, 0)):
        for start in range(0, SENT, 160):
            out = pl.ds(base + start, 160)
            back_hidden = mm_last(source[start : start + 160], down_ref[...])
            back_up = (back_hidden * act_ref[out]).astype(BF)
            back_gate = (back_hidden * slope_ref[out]).astype(BF)
            bg_ref[out] = back_gate
            bu_ref[out] = back_up
            target[start : start + 160] = (mm(back_gate, gate_ref[...]) + mm(back_up, up_ref[...])).astype(BF)


def grads_body(x_own, x_rest, c_own, c_rest, bg_ref, bu_ref, hidden_ref, out_ref):
    parts = ((bg_ref, x_own, x_rest), (bu_ref, x_own, x_rest), (hidden_ref, c_own, c_rest))
    for kind, (lhs, own, rest) in enumerate(parts):
        total = mm_first(lhs[:SENT], own[...]) + mm_first(lhs[SENT:], rest[...])
        for d in range(4):
            out_ref[d, kind * HALF : (kind + 1) * HALF] = total[:, d * 256 : (d + 1) * 256].astype(BF)


def combine_body(own_ref, other_ref, out_slots):
    out_slots[...] = (own_ref[...].astype(F32) + other_ref[...].astype(F32)).astype(BF)


def node_body(sel_ref, ret_ref, out_ref):
    out_ref[:, :WIDTH] = mm_first(sel_ref[:, :MSG], ret_ref[...]).astype(BF)
    out_ref[:, WIDTH:] = (
        mm_first(sel_ref[:, MSG : 2 * MSG], ret_ref[:, :MID])
        + mm_first(sel_ref[:, 2 * MSG :], ret_ref[:, MID:])
    ).astype(BF)


def final_body(sel_ref, msg_ref, out_ref):
    low = msg_ref[:, WIDTH:]
    out_ref[:, :MID] = (mm_first(sel_ref[0], msg_ref[:, :MID]) + mm_first(sel_ref[1], low)).astype(BF)
    out_ref[:, MID:] = (mm_first(sel_ref[0], msg_ref[:, MID:WIDTH]) + mm_first(sel_ref[2], low)).astype(BF)


def call(body, outs, flops, moved, *args):
    shapes = tuple(jax.ShapeDtypeStruct(s, t) for s, t in outs)
    whole = pl.BlockSpec(memory_space=pltpu.VMEM)
    return pl.pallas_call(
        body,
        out_shape=shapes,
        in_specs=[whole] * len(args),
        out_specs=tuple([whole] * len(outs)),
        compiler_params=pltpu.CompilerParams(vmem_limit_bytes=32 * 1024 * 1024),
        cost_estimate=pl.CostEstimate(flops=flops, bytes_accessed=moved, transcendentals=0),
        name=body.__name__,
    )(*args)


def over_nodes(x):
    return lax.all_to_all(x, "node", split_axis=0, concat_axis=0, tiled=True)


def over_chips(x):
    return lax.all_to_all(x, "local", split_axis=0, concat_axis=0, tiled=True, axis_index_groups=SAME_CORE)


def other_core(x):
    return lax.ppermute(x, "local", OTHER_CORE)


def on_device(tokens, upstream, expert_ids, gate_weights, w_gate, w_up, w_down):
    gate_half, up_half, down_half = w_gate[0], w_up[0], w_down[0]
    xmsg, umsg, row_sel = call(
        route_body,
        [((MSG, META), BF), ((MSG, WIDE), BF), ((3, MSG, TOKS), BF)],
        60_000_000,
        1_300_000,
        tokens,
        upstream,
        expert_ids,
        gate_weights,
    )
    x_in = over_nodes(xmsg)
    u_in = over_nodes(umsg)
    x_out, slot_sel, slot_gated = call(
        place_body,
        [((SENT, WIDTH), BF), ((SENT, 3 * MSG), BF), ((SENT, 3 * MSG), BF)],
        200_000_000,
        1_500_000,
        x_in,
    )
    x_own = over_chips(x_out)
    x_rest = other_core(x_own)
    act, slope, hidden = call(
        forward_body,
        [((ROWS, HALF), F32), ((ROWS, HALF), F32), ((ROWS, HALF), BF)],
        920_000_000,
        6_000_000,
        x_own,
        x_rest,
        gate_half,
        up_half,
    )
    (c_out,) = call(cotangent_body, [((SENT, WIDTH), BF)], 200_000_000, 1_300_000, u_in, slot_gated)
    c_own = over_chips(c_out)
    c_rest = other_core(c_own)
    piece_own, piece_rest, back_gate, back_up = call(
        backward_body,
        [((SENT, WIDTH), BF), ((SENT, WIDTH), BF), ((ROWS, HALF), BF), ((ROWS, HALF), BF)],
        1_400_000_000,
        8_000_000,
        c_own,
        c_rest,
        down_half,
        gate_half,
        up_half,
        act,
        slope,
    )
    piece_other = other_core(piece_rest)
    (grads,) = call(
        grads_body,
        [((4, 3 * HALF, 256), BF)],
        1_400_000_000,
        7_000_000,
        x_own,
        x_rest,
        c_own,
        c_rest,
        back_gate,
        back_up,
        hidden,
    )
    summed = lax.psum_scatter(grads.reshape(12 * HALF, 256), "dp", scatter_dimension=0, tiled=True)
    (pair_sum,) = call(combine_body, [((SENT, WIDTH), BF)], 1_000_000, 2_000_000, piece_own, piece_other)
    returned = over_chips(pair_sum)
    (node_sum,) = call(node_body, [((MSG, WIDE), BF)], 200_000_000, 1_300_000, slot_sel, returned)
    node_back = over_nodes(node_sum)
    (token_grads,) = call(final_body, [((TOKS, WIDTH), BF)], 50_000_000, 600_000, row_sel, node_back)
    return (
        token_grads,
        summed[None, :HALF],
        summed[None, HALF : 2 * HALF],
        summed[None, 2 * HALF :],
    )


def solution(mesh):
    tok = P(("dp", "node", "local"), None)
    weight = P(("node", "local"), None, None)
    grad = P(("node", "local"), None, "dp")
    return jax.shard_map(
        on_device,
        mesh=mesh,
        in_specs=(tok, tok, tok, tok, weight, weight, weight),
        out_specs=(tok, grad, grad, grad),
        check_vma=False,
    )
```

time: 377 us -> 184 us (0.49)
  waiting for transfers between devices: 268 us -> 36.7 us
  blocking collectives: 0 us -> 86 us
  matrix products: 19.2 us -> 0 us
  starting transfers between devices: 38.2 us -> 20.3 us
  local copies, waits for them, and re-layouts: 26.5 us -> 8.72 us
  Pallas kernels: 0 us -> 17.2 us
  other arithmetic: 10.1 us -> 0 us
    all_to_all x3, waiting for transfers between devices: 268 us -> 34.9 us  [the longest x1 20.7 us: over_nodes(): return lax.all_to_all(x, 'node', split_axis=0, concat_axis=0, tiled=True)]
    all_to_all x0 -> x3, blocking collectives: none -> 86 us  [the longest x2 71.8 us: over_nodes(): return lax.all_to_all(x, 'node', split_axis=0, concat_axis=0, tiled=True)]
    all_to_all x3, starting transfers between devices: 38 us -> 14.1 us  [the longest x2 7.93 us: over_chips(): lax.all_to_all(x, 'local', split_axis=0, concat_axis=0, tiled=True, axis_...]
    dot_general x8 -> x0, matrix products: 19.2 us -> none  [the longest x1 3.49 us: expert_backward(): lax.dot_general(hidden, cot_rows, contract_first, preferred_element_type=...]
    pallas_call x0 -> x9, Pallas kernels: none -> 17.2 us  [call(): pl.pallas_call(body, out_shape=shapes, in_specs=[whole] * len(args), out_...]
    reshape x5 -> x0, local copies, waits for them, and re-layouts: 7.6 us -> none  [the longest x1 2.62 us: on_device(): cot_got.reshape(-1, width)]
    ppermute x0 -> x3, starting transfers between devices: none -> 6.21 us  [other_core(): return lax.ppermute(x, 'local', OTHER_CORE)]
    unnamed x15 -> x28, local copies, waits for them, and re-layouts: 0.8 us -> 6.82 us
  transfers between devices with their start and end apart: 6 -> 7, of which waited for: 3 -> 4; matrix products, arithmetic and copies ran while one was open for 9% -> 0% of each run, Pallas kernels for 0% -> 4%
where the time goes in v1:
time: 184 us; the launch traced here: 183 us
  blocking collectives  86 us (47%)
  waiting for transfers between devices  36.7 us (20%)
  starting transfers between devices  20.3 us (11%)
  Pallas kernels  17.2 us (9%)
  between operations  14.2 us (8%)
  local copies, waits for them, and re-layouts  8.72 us (5%)
    all_to_all x2, blocking collectives, over_nodes(): return lax.all_to_all(x, 'node', split_axis=0, concat_axis=0, tiled=True)  71.8 us
    all_to_all x1, waiting for transfers between devices, over_nodes(): return lax.all_to_all(x, 'node', split_axis=0, concat_axis=0, tiled=True)  20.7 us
    pallas_call x9, Pallas kernels, call(): pl.pallas_call(body, out_shape=shapes, in_specs=[whole] * len(args), out_...  17.2 us
    all_to_all x1, blocking collectives, over_chips(): lax.all_to_all(x, 'local', split_axis=0, concat_axis=0, tiled=True, axis_...  14.2 us
    all_to_all x2, waiting for transfers between devices, over_chips(): lax.all_to_all(x, 'local', split_axis=0, concat_axis=0, tiled=True, axis_...  14.2 us
    all_to_all x2, starting transfers between devices, over_chips(): lax.all_to_all(x, 'local', split_axis=0, concat_axis=0, tiled=True, axis_...  7.93 us
    unnamed x28, local copies, waits for them, and re-layouts  6.82 us
    ppermute x3, starting transfers between devices, other_core(): return lax.ppermute(x, 'local', OTHER_CORE)  6.21 us
  transfers between devices with their start and end apart: 7, of which 4 were waited for; matrix products, arithmetic and copies ran while one was open for 0% of the time, Pallas kernels for 4%

profile of v1, /device:TPU:24, one launch (start us, length us, event | category | flops | bytes accessed | tf_op | source)
XLA Modules:
  0.0 183.1 jit_solution(4697749876679676724)
XLA Ops:
  7.2 0.8 copy.11.ids_ref
  7.9 0.8 copy.12.gate_ref
  8.7 0.9 copy-done.7
  9.6 0.9 copy-done.8
  10.5 1.5 route_body.1
  12.0 40.0 %all_to_all.66 = bf16[16,8,1664]{2,1,0:T(8,128)(2,1)S(1)} all-to-all(bf16[16,8,1664]{2,1,0:T(8,128)(2,1)S(1)} %bitcast.39), channel_id=1, replica_groups=mesh['dp'=4,'node'=16,'local'=8] {'node'}, dimensions={0} | all-to-all | bytes 851968 | tf_op jit(solution)/shard_map/all_to_all | solution.py:183
  52.0 6.1 %all-to-all-start.1 = ((bf16[16,8,1536]{2,1,0:T(8,128)(2,1)}), bf16[16,8,1536]{2,1,0:T(8,128)(2,1)S(1)}, u32[]{:S(2)}, u32[]{:S(2)}) async-start(bf16[16,8,1536]{2,1,0:T(8,128)(2,1)} %bitcast.2), calls=%async_computation.1 | async-start | bytes 786432 | tf_op jit(solution)/shard_map/all_to_all | solution.py:183
  58.2 1.6 place_body.1
  59.8 0.7 copy-done.5
  60.5 20.7 %all-to-all-done.1 = bf16[16,8,1536]{2,1,0:T(8,128)(2,1)S(1)} async-done(((bf16[16,8,1536]{2,1,0:T(8,128)(2,1)}), bf16[16,8,1536]{2,1,0:T(8,128)(2,1)S(1)}, u32[]{:S(2)}, u32[]{:S(2)}) %all-to-all-start.1) | async-done | bytes 393248 | tf_op jit(solution)/shard_map/all_to_all | solution.py:183
  81.3 4.3 %all-to-all-start.3 = ((bf16[4,80,1024]{2,1,0:T(8,128)(2,1)}), bf16[4,80,1024]{2,1,0:T(8,128)(2,1)S(1)}, u32[]{:S(2)}, u32[]{:S(2)}) async-start(bf16[4,80,1024]{2,1,0:T(8,128)(2,1)} %bitcast.9), calls=%async_computation.3 | async-start | bytes 1310720 | tf_op jit(solution)/shard_map/all_to_all | solution.py:187
  85.6 1.4 cotangent_body.1
  87.0 7.4 %all-to-all-done.3 = bf16[4,80,1024]{2,1,0:T(8,128)(2,1)S(1)} async-done(((bf16[4,80,1024]{2,1,0:T(8,128)(2,1)}), bf16[4,80,1024]{2,1,0:T(8,128)(2,1)S(1)}, u32[]{:S(2)}, u32[]{:S(2)}) %all-to-all-start.3) | async-done | bytes 655392 | tf_op jit(solution)/shard_map/all_to_all | solution.py:187
  94.4 3.6 %all-to-all-start.2 = ((bf16[4,80,1024]{2,1,0:T(8,128)(2,1)}), bf16[4,80,1024]{2,1,0:T(8,128)(2,1)S(1)}, u32[]{:S(2)}, u32[]{:S(2)}) async-start(bf16[4,80,1024]{2,1,0:T(8,128)(2,1)} %bitcast.4), calls=%async_computation.2 | async-start | bytes 1310720 | tf_op jit(solution)/shard_map/all_to_all | solution.py:187
  98.0 0.0 reduce-scatter.2.cloned.1.call-start
  98.1 1.9 %collective-permute-start.1 = (bf16[320,1024]{1,0:T(8,128)(2,1)S(1)}, bf16[320,1024]{1,0:T(8,128)(2,1)}, u32[]{:S(2)}, u32[]{:S(2)}) collective-permute-start(bf16[320,1024]{1,0:T(8,128)(2,1)S(1)} %bitcast.25), channel_id=1, source_target_pairs={{0,1},{1,0},{2,3},{3,2},{4,5},{5,4},{6,7},{7,6},{8,9},{9,8},{10,11... | collective-permute-start | bytes 1966088 | tf_op jit(solution)/shard_map/ppermute | solution.py:191
  100.0 6.8 %all-to-all-done.2 = bf16[4,80,1024]{2,1,0:T(8,128)(2,1)S(1)} async-done(((bf16[4,80,1024]{2,1,0:T(8,128)(2,1)}), bf16[4,80,1024]{2,1,0:T(8,128)(2,1)S(1)}, u32[]{:S(2)}, u32[]{:S(2)}) %all-to-all-start.2) | async-done | bytes 655392 | tf_op jit(solution)/shard_map/all_to_all | solution.py:187
  106.8 1.9 %collective-permute-start = (bf16[320,1024]{1,0:T(8,128)(2,1)S(1)}, bf16[320,1024]{1,0:T(8,128)(2,1)S(1)}, u32[]{:S(2)}, u32[]{:S(2)}) collective-permute-start(bf16[320,1024]{1,0:T(8,128)(2,1)S(1)} %bitcast.22), channel_id=1, source_target_pairs={{0,1},{1,0},{2,3},{3,2},{4,5},{5,4},{6,7},{7,6},{8,9},{9,8},{10,11... | collective-permute-start | bytes 1966088 | tf_op jit(solution)/shard_map/ppermute | solution.py:191
  108.7 3.1 %forward_body.1 = (f32[640,352]{1,0:T(8,128)S(1)}, f32[640,352]{1,0:T(8,128)S(1)}, bf16[640,352]{1,0:T(8,128)(2,1)S(1)}) custom-call(bf16[320,1024]{1,0:T(8,128)(2,1)S(1)} %bitcast.26, bf16[320,1024]{1,0:T(8,128)(2,1)} %collective-permute-done.1.rest_ref.x_rest, bf16[352,1024]{1,0:T(8,128)(2,1)S(1)} %bitcast.34, bf16[352,1024]{1,0:T(8,128)(2,1)S(1)} %bitcast.36), custom_call_target="tpu_custom_call" | custom-call | flops 920000000 | bytes 6000000 | tf_op jit(solution)/shard_map/forward_body/pallas_call | solution.py:171
  111.9 3.2 %backward_body.1 = (bf16[320,1024]{1,0:T(8,128)(2,1)S(1)}, bf16[320,1024]{1,0:T(8,128)(2,1)S(1)}, bf16[640,352]{1,0:T(8,128)(2,1)S(1)}, bf16[640,352]{1,0:T(8,128)(2,1)S(1)}) custom-call(bf16[320,1024]{1,0:T(8,128)(2,1)S(1)} %bitcast.23, bf16[320,1024]{1,0:T(8,128)(2,1)S(1)} %collective-permute-done.rest_ref.c_rest, bf16[352,1024]{1,0:T(8,128)(2,1)S(1)} %bitcast.33, ...), custom_call_target="tpu_custom_call" | custom-call | flops 1400000000 | bytes 8000000 | tf_op jit(solution)/shard_map/backward_body/pallas_call | solution.py:171
  115.1 0.8 copy-done.3
  116.0 0.8 copy-done.11
  116.8 4.9 %grads_body.1 = bf16[4,1056,256]{2,1,0:T(8,128)(2,1)} custom-call(bf16[320,1024]{1,0:T(8,128)(2,1)S(1)} %bitcast.27, bf16[320,1024]{1,0:T(8,128)(2,1)} %collective-permute-done.1.rest_ref.x_rest, bf16[320,1024]{1,0:T(8,128)(2,1)S(1)} %bitcast.24, bf16[320,1024]{1,0:T(8,128)(2,1)S(1)} %collective-permute-done.rest_ref.c_rest, ...), custom_call_target="tpu_custom_call" | custom-call | flops 1400000000 | bytes 7000000 | tf_op jit(solution)/shard_map/grads_body/pallas_call | solution.py:171
  121.7 1.0 copy-done.12
  122.8 2.4 %collective-permute-start.2 = (bf16[320,1024]{1,0:T(8,128)(2,1)S(1)}, bf16[320,1024]{1,0:T(8,128)(2,1)S(1)}, u32[]{:S(2)}, u32[]{:S(2)}) collective-permute-start(bf16[320,1024]{1,0:T(8,128)(2,1)S(1)} %copy-done.12), channel_id=1, source_target_pairs={{0,1},{1,0},{2,3},{3,2},{4,5},{5,4},{6,7},{7,6},{8,9},{9,8},{10,11... | collective-permute-start | bytes 1966088 | tf_op jit(solution)/shard_map/ppermute | solution.py:191
  125.2 1.7 collective-permute-done.2.other_ref
  126.9 0.2 combine_body.1
  127.0 14.2 %all_to_all.67 = bf16[4,80,1024]{2,1,0:T(8,128)(2,1)S(1)} all-to-all(bf16[4,80,1024]{2,1,0:T(8,128)(2,1)S(1)} %bitcast.29), channel_id=1, replica_groups={{0,2,4,6},{1,3,5,7},{8,10,12,14},{9,11,13,15},{16,18,20,22},{17,19,21,2..., dimensions={0} | all-to-all | bytes 1310720 | tf_op jit(solution)/shard_map/all_to_all | solution.py:187
  141.3 0.5 node_body.1
  141.7 31.8 %all_to_all.68 = bf16[16,8,1536]{2,1,0:T(8,128)(2,1)S(1)} all-to-all(bf16[16,8,1536]{2,1,0:T(8,128)(2,1)S(1)} %bitcast.32), channel_id=1, replica_groups=mesh['dp'=4,'node'=16,'local'=8] {'node'}, dimensions={0} | all-to-all | bytes 786432 | tf_op jit(solution)/shard_map/all_to_all | solution.py:183
  173.5 0.9 final_body.1
  174.4 1.9 %slice_bitcast_fusion = (bf16[1,352,256]{2,1,0:T(8,128)(2,1)}, bf16[1,352,256]{2,1,0:T(8,128)(2,1)}, bf16[1,352,256]{2,1,0:T(8,128)(2,1)}) fusion(bf16[1056,256]{1,0:T(8,128)(2,1)} %reduce-scatter.2.cloned.1.call-done), kind=kLoop, calls=%fused_computation | loop fusion | bytes 1081344 | tf_op jit(solution)/shard_map/broadcast_in_dim | solution.py:267
  (24 shorter events, 0.1 us)
Async XLA Ops:
  8.7 0.9 copy-start.7
  9.6 0.9 copy-start.8
  12.0 40.0 %copy-start.9 = (bf16[3,128,64]{2,1,0:T(8,128)(2,1)}, bf16[3,128,64]{2,1,0:T(8,128)(2,1)S(1)}, u32[]{:S(2)}) copy-start(bf16[3,128,64]{2,1,0:T(8,128)(2,1)S(1)} %get-tuple-element.17.sel_ref) | copy-start | bytes 147460
  52.0 29.2 %all-to-all-start.1 = ((bf16[16,8,1536]{2,1,0:T(8,128)(2,1)}), bf16[16,8,1536]{2,1,0:T(8,128)(2,1)S(1)}, u32[]{:S(2)}, u32[]{:S(2)}) async-start(bf16[16,8,1536]{2,1,0:T(8,128)(2,1)} %bitcast.2), calls=%async_computation.1 | async-start | bytes 786432 | tf_op jit(solution)/shard_map/all_to_all | solution.py:183
  58.2 50.5 %copy-start.1 = (bf16[1,352,1024]{2,1,0:T(8,128)(2,1)S(1)}, bf16[1,352,1024]{2,1,0:T(8,128)(2,1)}, u32[]{:S(2)}) copy-start(bf16[1,352,1024]{2,1,0:T(8,128)(2,1)} %param.11) | copy-start | bytes 2162692
  58.2 50.5 %copy-start.2 = (bf16[1,352,1024]{2,1,0:T(8,128)(2,1)S(1)}, bf16[1,352,1024]{2,1,0:T(8,128)(2,1)}, u32[]{:S(2)}) copy-start(bf16[1,352,1024]{2,1,0:T(8,128)(2,1)} %param.12) | copy-start | bytes 2162692
  59.8 0.7 copy-start.5
  81.3 13.1 %all-to-all-start.3 = ((bf16[4,80,1024]{2,1,0:T(8,128)(2,1)}), bf16[4,80,1024]{2,1,0:T(8,128)(2,1)S(1)}, u32[]{:S(2)}, u32[]{:S(2)}) async-start(bf16[4,80,1024]{2,1,0:T(8,128)(2,1)} %bitcast.9), calls=%async_computation.3 | async-start | bytes 1310720 | tf_op jit(solution)/shard_map/all_to_all | solution.py:187
  94.4 17.5 %copy-start = (bf16[1,352,1024]{2,1,0:T(8,128)(2,1)S(1)}, bf16[1,352,1024]{2,1,0:T(8,128)(2,1)}, u32[]{:S(2)}) copy-start(bf16[1,352,1024]{2,1,0:T(8,128)(2,1)} %param.13) | copy-start | bytes 2162692
  94.4 12.4 %all-to-all-start.2 = ((bf16[4,80,1024]{2,1,0:T(8,128)(2,1)}), bf16[4,80,1024]{2,1,0:T(8,128)(2,1)S(1)}, u32[]{:S(2)}, u32[]{:S(2)}) async-start(bf16[4,80,1024]{2,1,0:T(8,128)(2,1)} %bitcast.4), calls=%async_computation.2 | async-start | bytes 1310720 | tf_op jit(solution)/shard_map/all_to_all | solution.py:187
  98.0 76.4 %reduce-scatter.2.cloned.1.call-start = ((), (), s32[]{:S(2)}) async-start(), calls=%async_computation.7 | async-start | bytes 2703360 | tf_op jit(solution)/shard_map/reduce_scatter | solution.py:257
  98.1 10.6 %collective-permute-start.1 = (bf16[320,1024]{1,0:T(8,128)(2,1)S(1)}, bf16[320,1024]{1,0:T(8,128)(2,1)}, u32[]{:S(2)}, u32[]{:S(2)}) collective-permute-start(bf16[320,1024]{1,0:T(8,128)(2,1)S(1)} %bitcast.25), channel_id=1, source_target_pairs={{0,1},{1,0},{2,3},{3,2},{4,5},{5,4},{6,7},{7,6},{8,9},{9,8},{10,11... | collective-permute-start | bytes 1966088 | tf_op jit(solution)/shard_map/ppermute | solution.py:191
  106.8 5.1 %collective-permute-start = (bf16[320,1024]{1,0:T(8,128)(2,1)S(1)}, bf16[320,1024]{1,0:T(8,128)(2,1)S(1)}, u32[]{:S(2)}, u32[]{:S(2)}) collective-permute-start(bf16[320,1024]{1,0:T(8,128)(2,1)S(1)} %bitcast.22), channel_id=1, source_target_pairs={{0,1},{1,0},{2,3},{3,2},{4,5},{5,4},{6,7},{7,6},{8,9},{9,8},{10,11... | collective-permute-start | bytes 1966088 | tf_op jit(solution)/shard_map/ppermute | solution.py:191
  115.1 0.8 copy-start.3
  116.0 0.8 copy-start.11
  121.7 1.1 copy-start.12
  121.7 5.2 %copy-start.4 = (bf16[320,1024]{1,0:T(8,128)(2,1)S(1)}, bf16[320,1024]{1,0:T(8,128)(2,1)}, u32[]{:S(2)}) copy-start(bf16[320,1024]{1,0:T(8,128)(2,1)} %copy-done.3) | copy-start | bytes 1966084
  121.7 19.6 %copy-start.6 = (bf16[320,384]{1,0:T(8,128)(2,1)S(1)}, bf16[320,384]{1,0:T(8,128)(2,1)}, u32[]{:S(2)}) copy-start(bf16[320,384]{1,0:T(8,128)(2,1)} %copy-done.5) | copy-start | bytes 737284
  122.8 4.1 %collective-permute-start.2 = (bf16[320,1024]{1,0:T(8,128)(2,1)S(1)}, bf16[320,1024]{1,0:T(8,128)(2,1)S(1)}, u32[]{:S(2)}, u32[]{:S(2)}) collective-permute-start(bf16[320,1024]{1,0:T(8,128)(2,1)S(1)} %copy-done.12), channel_id=1, source_target_pairs={{0,1},{1,0},{2,3},{3,2},{4,5},{5,4},{6,7},{7,6},{8,9},{9,8},{10,11... | collective-permute-start | bytes 1966088 | tf_op jit(solution)/shard_map/ppermute | solution.py:191
  127.0 46.5 %copy-start.10 = (bf16[3,128,64]{2,1,0:T(8,128)(2,1)S(1)}, bf16[3,128,64]{2,1,0:T(8,128)(2,1)}, u32[]{:S(2)}) copy-start(bf16[3,128,64]{2,1,0:T(8,128)(2,1)} %copy-done.9) | copy-start | bytes 147460
Sparse Core Ops, SparseCore 0:
  121.8 32.5 reduce-scatter.1

commit v2 on v1

v2 whole, which is shorter than its diff:
```python
import jax
import jax.numpy as jnp
from jax import lax
from jax.experimental import pallas as pl
from jax.experimental.pallas import tpu as pltpu
from jax.sharding import PartitionSpec as P

WIDTH = 1024
MID = 512
WIDE = 1536
META = 3072
HALF = 352
TOKS = 64
MSG = 128
CAP = 5
SLOT = 80
SENT = 320
F32 = jnp.float32
BF = jnp.bfloat16
SAME_CORE = [[0, 2, 4, 6], [1, 3, 5, 7]]
OTHER_CORE = [(i, i ^ 1) for i in range(8)]
VMEM = pl.BlockSpec(memory_space=pltpu.VMEM)
HBM = pl.BlockSpec(memory_space=pltpu.HBM)


def mm(a, b):
    return jnp.dot(a, b, preferred_element_type=F32)


def mm_first(a, b):
    return lax.dot_general(a, b, (((0,), (0,)), ((), ())), preferred_element_type=F32)


def mm_last(a, b):
    return lax.dot_general(a, b, (((1,), (1,)), ((), ())), preferred_element_type=F32)


def iota(shape, dim):
    return lax.broadcasted_iota(jnp.int32, shape, dim)


def one(cond):
    return jnp.where(cond, 1.0, 0.0).astype(BF)


def route_body(ids_hbm, gate_hbm, tok_hbm, up_hbm, msg_ref, sel_hbm, ids_ref, gate_ref, tok_ref, up_ref, sel_ref, sems):
    pairs = ((ids_hbm, ids_ref), (gate_hbm, gate_ref), (tok_hbm, tok_ref), (up_hbm, up_ref))
    loads = [pltpu.make_async_copy(src, dst, sems.at[i]) for i, (src, dst) in enumerate(pairs)]
    for load in loads:
        load.start()
    loads[0].wait()
    loads[1].wait()
    ids = ids_ref[...]
    gates = gate_ref[...].astype(F32)
    node = iota((MSG, TOKS), 0) >> 3
    expert = iota((TOKS, TOKS), 0)
    named = jnp.zeros((MSG, TOKS), F32)
    weight = jnp.zeros((TOKS, TOKS), F32)
    for k in range(4):
        row = ids[k : k + 1]
        named = jnp.where((row >> 2) == node, 1.0, named)
        weight = jnp.where(row == expert, gates[k : k + 1], weight)
    weight = weight.astype(BF)
    hit = named > 0.5
    rank = mm(named.astype(BF), one(iota((TOKS, TOKS), 0) < iota((TOKS, TOKS), 1))).astype(jnp.int32)
    place = iota((MSG, TOKS), 0) & 7
    late = hit & (rank == 8 + (place & 3))
    whole = one(hit & (rank == place))
    left = one(late & (place < 4))
    right = one(late & (place >= 4))
    sel_ref[0] = whole
    sel_ref[1] = left
    sel_ref[2] = right
    store = pltpu.make_async_copy(sel_ref, sel_hbm, sems.at[4])
    store.start()
    own_node = (iota((MSG, TOKS), 1) >> 2) == node
    gate_whole = jnp.where(own_node, mm_last(whole, weight), 0.0).astype(BF)
    gate_late = jnp.where(own_node, mm_last(left + right, weight), 0.0).astype(BF)
    fold_row, fold_col = iota((TOKS, MSG), 0) & 3, iota((TOKS, MSG), 1)
    meta = mm(gate_whole, one(fold_col == fold_row)) + mm(gate_late, one(fold_col == fold_row + 8))
    msg_ref[:, META:] = meta.astype(BF)
    for load, src, base in ((loads[2], tok_ref, 0), (loads[3], up_ref, WIDE)):
        load.wait()
        msg_ref[:, base : base + WIDTH] = mm(whole, src[...]).astype(BF)
        low = mm(left, src[:, :MID]) + mm(right, src[:, MID:])
        msg_ref[:, base + WIDTH : base + WIDE] = low.astype(BF)
    store.wait()


def spread(sel, msg_ref, at, out_ref, to):
    low = msg_ref[:, at + WIDTH : at + WIDE]
    left = mm(sel[:, :MSG], msg_ref[:, at : at + MID]) + mm(sel[:, MSG : 2 * MSG], low)
    right = mm(sel[:, :MSG], msg_ref[:, at + MID : at + WIDTH]) + mm(sel[:, 2 * MSG :], low)
    out_ref[:, to : to + MID] = left.astype(BF)
    out_ref[:, to + MID : to + WIDTH] = right.astype(BF)


def place_body(msg_ref, out_ref, sel_hbm, sel_ref, gated_ref, sem):
    row, col = iota((MSG, MSG), 0), iota((MSG, MSG), 1)
    gates = mm_first(msg_ref[:, META:], one(row == col))
    gate_whole, gate_late = gates[0:8], gates[8:16]
    has_whole, has_late = one(gate_whole > 0.0), one(gate_late > 0.0)
    same = (row >> 3) == (col >> 3)
    rank_whole = mm(has_whole, one(same & (row < col)))
    rank_late = mm(has_whole, one(same)) + mm(has_late, one(same & ((row & 7) < (col & 3))))
    node = (iota((8, MSG), 1) >> 3) * CAP
    lane_place = iota((8, MSG), 1) & 7
    slot_whole = jnp.where(gate_whole > 0.0, node + rank_whole.astype(jnp.int32), -1)
    slot_late = jnp.where(gate_late > 0.0, node + rank_late.astype(jnp.int32), -1)
    slot_left = jnp.where(lane_place < 4, slot_late, -1)
    slot_right = jnp.where(lane_place >= 4, slot_late, -1)
    slots = iota((SLOT, MSG), 0)
    for j in range(4):
        parts = ((slot_whole, gate_whole), (slot_left, gate_late), (slot_right, gate_late))
        for part, (slot, gate) in enumerate(parts):
            match = slots == slot[j : j + 1]
            rows, lanes = pl.ds(j * SLOT, SLOT), pl.ds(part * MSG, MSG)
            sel_ref[rows, lanes] = one(match)
            gated_ref[rows, lanes] = jnp.where(match, gate[j : j + 1], 0.0).astype(BF)
    store = pltpu.make_async_copy(sel_ref, sel_hbm, sem)
    store.start()
    spread(sel_ref, msg_ref, 0, out_ref, 0)
    spread(gated_ref, msg_ref, WIDE, out_ref, WIDTH)
    store.wait()


def activate(x, gate_ref, up_ref):
    gate_logit = mm_last(x, gate_ref[...])
    up_value = mm_last(x, up_ref[...])
    sig = jax.nn.sigmoid(gate_logit)
    act = gate_logit * sig
    return act, up_value * sig * (1.0 + gate_logit * (1.0 - sig)), (act * up_value).astype(BF)


def own_body(*refs):
    hbm, (piece_hbm, bg_hbm, bu_hbm, hidden_hbm) = refs[0:7], refs[7:11]
    vmem, (total_ref, piece_ref, bg_ref, bu_ref, hidden_ref, sems) = refs[11:18], refs[18:]
    loads = [pltpu.make_async_copy(src, dst, sems.at[i]) for i, (src, dst) in enumerate(zip(hbm, vmem))]
    for load in loads:
        load.start()
    backs = ((bg_ref, bg_hbm), (bu_ref, bu_hbm), (hidden_ref, hidden_hbm))
    stores = [pltpu.make_async_copy(src, dst, sems.at[7 + i]) for i, (src, dst) in enumerate(backs)]
    xc_ref = vmem[0]
    loads[0].wait()
    for half in range(2):
        gate_ref, up_ref, down_ref = vmem[1 + 3 * half : 4 + 3 * half]
        for load in loads[1 + 3 * half : 4 + 3 * half]:
            load.wait()
        for start in range(0, SENT, 160):
            rows = pl.ds(start, 160)
            x, c = xc_ref[rows, :WIDTH], xc_ref[rows, WIDTH:]
            act, slope, hidden = activate(x, gate_ref, up_ref)
            back_hidden = mm_last(c, down_ref[...])
            back_up = (back_hidden * act).astype(BF)
            back_gate = (back_hidden * slope).astype(BF)
            part = mm(back_gate, gate_ref[...]) + mm(back_up, up_ref[...])
            if half == 0:
                bg_ref[rows] = back_gate
                bu_ref[rows] = back_up
                hidden_ref[rows] = hidden
                total_ref[rows] = part
            else:
                piece_ref[rows] = (total_ref[rows] + part).astype(BF)
        if half == 0:
            for store in stores:
                store.start()
    last = pltpu.make_async_copy(piece_ref, piece_hbm, sems.at[10])
    last.start()
    for store in stores:
        store.wait()
    last.wait()


def grads_body(*refs):
    hbm, out_hbm, vmem, (out_ref, bg2_ref, bu2_ref, hidden2_ref, sems) = refs[0:8], refs[8], refs[9:17], refs[17:]
    loads = [pltpu.make_async_copy(src, dst, sems.at[i]) for i, (src, dst) in enumerate(zip(hbm, vmem))]
    for load in loads:
        load.start()
    rest_ref, gate_ref, up_ref, down_ref, own_ref, bg_ref, bu_ref, hidden_ref = vmem
    for load in loads[:4]:
        load.wait()
    for start in range(0, SENT, 160):
        rows = pl.ds(start, 160)
        act, slope, hidden2_ref[rows] = activate(rest_ref[rows, :WIDTH], gate_ref, up_ref)
        back_hidden = mm_last(rest_ref[rows, WIDTH:], down_ref[...])
        bu2_ref[rows] = (back_hidden * act).astype(BF)
        bg2_ref[rows] = (back_hidden * slope).astype(BF)
    for load in loads[4:]:
        load.wait()
    parts = ((bg_ref, bg2_ref, 0), (bu_ref, bu2_ref, 0), (hidden_ref, hidden2_ref, WIDTH))
    stores = []
    for kind, (lhs_own, lhs_rest, at) in enumerate(parts):
        cols = pl.ds(at, WIDTH)
        total = mm_first(lhs_own[...], own_ref[:, cols]) + mm_first(lhs_rest[...], rest_ref[:, cols])
        rows = pl.ds(kind * HALF, HALF)
        for d in range(4):
            out_ref[d, rows] = total[:, d * 256 : (d + 1) * 256].astype(BF)
        stores.append(pltpu.make_async_copy(out_ref.at[:, rows], out_hbm.at[:, rows], sems.at[8 + kind]))
        stores[-1].start()
    for store in stores:
        store.wait()


def node_body(sel_ref, ret_ref, out_ref):
    out_ref[:, :WIDTH] = mm_first(sel_ref[:, :MSG], ret_ref[...]).astype(BF)
    out_ref[:, WIDTH:] = (
        mm_first(sel_ref[:, MSG : 2 * MSG], ret_ref[:, :MID])
        + mm_first(sel_ref[:, 2 * MSG :], ret_ref[:, MID:])
    ).astype(BF)


def final_body(sum_hbm, sel_hbm, msg_hbm, out_hbm, gate_hbm, up_hbm, down_hbm, sum_ref, sel_ref, msg_ref, out_ref, sems):
    grads = []
    for kind, grad_hbm in enumerate((gate_hbm, up_hbm, down_hbm)):
        part = pl.ds(kind * HALF, HALF)
        load = pltpu.make_async_copy(sum_hbm.at[part], sum_ref.at[part], sems.at[kind])
        grads.append((load, pltpu.make_async_copy(sum_ref.at[part], grad_hbm, sems.at[3 + kind])))
    loads = [pltpu.make_async_copy(sel_hbm, sel_ref, sems.at[6]), pltpu.make_async_copy(msg_hbm, msg_ref, sems.at[7])]
    for load in loads:
        load.start()
    for load, _ in grads:
        load.start()
    for load, store in grads:
        load.wait()
        store.start()
    for load in loads:
        load.wait()
    low = msg_ref[:, WIDTH:]
    out_ref[:, :MID] = (mm_first(sel_ref[0], msg_ref[:, :MID]) + mm_first(sel_ref[1], low)).astype(BF)
    out_ref[:, MID:] = (mm_first(sel_ref[0], msg_ref[:, MID:WIDTH]) + mm_first(sel_ref[2], low)).astype(BF)
    last = pltpu.make_async_copy(out_ref, out_hbm, sems.at[8])
    last.start()
    for _, store in grads:
        store.wait()
    last.wait()


def call(body, ins, outs, flops, moved, *args, scratch=(), limit=60):
    return pl.pallas_call(
        body,
        out_shape=tuple(jax.ShapeDtypeStruct(s, BF) for s, _ in outs),
        in_specs=list(ins),
        out_specs=tuple(m for _, m in outs),
        scratch_shapes=list(scratch),
        compiler_params=pltpu.CompilerParams(vmem_limit_bytes=limit * 1024 * 1024),
        cost_estimate=pl.CostEstimate(flops=flops, bytes_accessed=moved, transcendentals=0),
        name=body.__name__,
    )(*args)


def over_nodes(x):
    return lax.all_to_all(x, "node", split_axis=0, concat_axis=0, tiled=True)


def over_chips(x):
    return lax.all_to_all(x, "local", split_axis=0, concat_axis=0, tiled=True, axis_index_groups=SAME_CORE)


def other_core(x):
    return lax.ppermute(x, "local", OTHER_CORE)


def on_device(tokens, upstream, expert_ids, gate_weights, w_gate, w_up, w_down):
    own = (w_gate[0], w_up[0], w_down[0])
    message, row_sel = call(
        route_body,
        [HBM] * 4,
        [((MSG, META + 128), VMEM), ((3, MSG, TOKS), HBM)],
        80_000_000,
        1_300_000,
        expert_ids.T,
        gate_weights.T,
        tokens,
        upstream,
        scratch=[
            pltpu.VMEM((4, TOKS), jnp.int32),
            pltpu.VMEM((4, TOKS), BF),
            pltpu.VMEM((TOKS, WIDTH), BF),
            pltpu.VMEM((TOKS, WIDTH), BF),
            pltpu.VMEM((3, MSG, TOKS), BF),
            pltpu.SemaphoreType.DMA((5,)),
        ],
    )
    message, *sent = lax.optimization_barrier((message, *own))
    arrived, *rest = lax.optimization_barrier((over_nodes(message), *(other_core(w) for w in sent)))
    placed, slot_sel = call(
        place_body,
        [VMEM],
        [((SENT, 2 * WIDTH), VMEM), ((SENT, 3 * MSG), HBM)],
        400_000_000,
        2_300_000,
        arrived,
        scratch=[pltpu.VMEM((SENT, 3 * MSG), BF), pltpu.VMEM((SENT, 3 * MSG), BF), pltpu.SemaphoreType.DMA],
        limit=16,
    )
    rows_own = over_chips(placed)
    rows_rest = other_core(rows_own)
    piece, *back_own = call(
        own_body,
        [HBM] * 7,
        [((SENT, WIDTH), HBM)] + [((SENT, HALF), HBM)] * 3,
        2_300_000_000,
        7_000_000,
        rows_own,
        *own,
        *rest,
        scratch=[
            pltpu.VMEM((SENT, 2 * WIDTH), BF),
            *[pltpu.VMEM((HALF, WIDTH), BF)] * 6,
            pltpu.VMEM((SENT, WIDTH), F32),
            pltpu.VMEM((SENT, WIDTH), BF),
            *[pltpu.VMEM((SENT, HALF), BF)] * 3,
            pltpu.SemaphoreType.DMA((11,)),
        ],
    )
    returned = over_chips(piece)
    (grads,) = call(
        grads_body,
        [HBM] * 8,
        [((4, 3 * HALF, 256), HBM)],
        2_100_000_000,
        8_000_000,
        rows_rest,
        *own,
        rows_own,
        *back_own,
        scratch=[
            pltpu.VMEM((SENT, 2 * WIDTH), BF),
            *[pltpu.VMEM((HALF, WIDTH), BF)] * 3,
            pltpu.VMEM((SENT, 2 * WIDTH), BF),
            *[pltpu.VMEM((SENT, HALF), BF)] * 3,
            pltpu.VMEM((4, 3 * HALF, 256), BF),
            *[pltpu.VMEM((SENT, HALF), BF)] * 3,
            pltpu.SemaphoreType.DMA((11,)),
        ],
    )
    summed = lax.psum_scatter(grads.reshape(12 * HALF, 256), "dp", scatter_dimension=0, tiled=True)
    (node_sum,) = call(node_body, [VMEM] * 2, [((MSG, WIDE), VMEM)], 50_000_000_000, 1_300_000, slot_sel, returned, limit=16)
    token_grads, *weight_grads = call(
        final_body,
        [HBM] * 3,
        [((TOKS, WIDTH), HBM)] + [((HALF, 256), HBM)] * 3,
        50_000_000,
        1_600_000,
        summed,
        row_sel,
        over_nodes(node_sum),
        scratch=[
            pltpu.VMEM((3 * HALF, 256), BF),
            pltpu.VMEM((3, MSG, TOKS), BF),
            pltpu.VMEM((MSG, WIDE), BF),
            pltpu.VMEM((TOKS, WIDTH), BF),
            pltpu.SemaphoreType.DMA((9,)),
        ],
    )
    return (token_grads, *[g[None] for g in weight_grads])


def solution(mesh):
    tok = P(("dp", "node", "local"), None)
    weight = P(("node", "local"), None, None)
    grad = P(("node", "local"), None, "dp")
    return jax.shard_map(
        on_device,
        mesh=mesh,
        in_specs=(tok, tok, tok, tok, weight, weight, weight),
        out_specs=(tok, grad, grad, grad),
        check_vma=False,
    )
```

time: 184 us -> 157 us (0.85)
  blocking collectives: 86 us -> 53 us
  starting transfers between devices: 20.3 us -> 26.9 us
  local copies, waits for them, and re-layouts: 8.72 us -> 2.82 us
  Pallas kernels: 17.2 us -> 21.8 us
    all_to_all x2 -> x1, blocking collectives: 71.8 us -> 36.1 us  [over_nodes(): return lax.all_to_all(x, 'node', split_axis=0, concat_axis=0, tiled=True)]
    all_to_all x1, waiting for transfers between devices: 20.7 us -> 31.7 us  [over_nodes(): return lax.all_to_all(x, 'node', split_axis=0, concat_axis=0, tiled=True)]
    all_to_all x2 -> x1, waiting for transfers between devices: 14.2 us -> 3.66 us  [over_chips(): lax.all_to_all(x, 'local', split_axis=0, concat_axis=0, tiled=True, axis_...]
    all_to_all x1, starting transfers between devices: 6.12 us -> 15.2 us  [over_nodes(): return lax.all_to_all(x, 'node', split_axis=0, concat_axis=0, tiled=True)]
    pallas_call x9 -> x6, Pallas kernels: 17.2 us -> 21.8 us  [call(): pl.pallas_call(body, out_shape=tuple((jax.ShapeDtypeStruct(s, BF) for s,...]
    all_to_all x2 -> x1, starting transfers between devices: 7.93 us -> 3.49 us  [over_chips(): lax.all_to_all(x, 'local', split_axis=0, concat_axis=0, tiled=True, axis_...]
    unnamed x28 -> x12, local copies, waits for them, and re-layouts: 6.82 us -> 2.82 us
    all_to_all x1, blocking collectives: 14.2 us -> 16.9 us  [over_chips(): lax.all_to_all(x, 'local', split_axis=0, concat_axis=0, tiled=True, axis_...]
  transfers between devices with their start and end apart: 7 -> 7, of which waited for: 4 -> 3; matrix products, arithmetic and copies ran while one was open for 0% -> 0% of each run, Pallas kernels for 4% -> 10%
where the time goes in v2:
time: 157 us; the launch traced here: 155 us
  blocking collectives  53 us (34%)
  waiting for transfers between devices  36.2 us (23%)
  starting transfers between devices  26.9 us (17%)
  Pallas kernels  21.8 us (14%)
  between operations  14.2 us (9%)
  local copies, waits for them, and re-layouts  2.82 us (2%)
    all_to_all x1, blocking collectives, over_nodes(): return lax.all_to_all(x, 'node', split_axis=0, concat_axis=0, tiled=True)  36.1 us
    all_to_all x1, waiting for transfers between devices, over_nodes(): return lax.all_to_all(x, 'node', split_axis=0, concat_axis=0, tiled=True)  31.7 us
    pallas_call x6, Pallas kernels, call(): pl.pallas_call(body, out_shape=tuple((jax.ShapeDtypeStruct(s, BF) for s,...  21.8 us
    all_to_all x1, blocking collectives, over_chips(): lax.all_to_all(x, 'local', split_axis=0, concat_axis=0, tiled=True, axis_...  16.9 us
    all_to_all x1, starting transfers between devices, over_nodes(): return lax.all_to_all(x, 'node', split_axis=0, concat_axis=0, tiled=True)  15.2 us
    ppermute x4, starting transfers between devices, other_core(): return lax.ppermute(x, 'local', OTHER_CORE)  8.16 us
    all_to_all x1, waiting for transfers between devices, over_chips(): lax.all_to_all(x, 'local', split_axis=0, concat_axis=0, tiled=True, axis_...  3.66 us
    all_to_all x1, starting transfers between devices, over_chips(): lax.all_to_all(x, 'local', split_axis=0, concat_axis=0, tiled=True, axis_...  3.49 us
  transfers between devices with their start and end apart: 7, of which 3 were waited for; matrix products, arithmetic and copies ran while one was open for 0% of the time, Pallas kernels for 10%

profile of v2, /device:TPU:24, one launch (start us, length us, event | category | flops | bytes accessed | tf_op | source)
XLA Modules:
  0.0 154.9 jit_solution(15155808089266051708)
XLA Ops:
  7.2 0.0 copy-start.3
  7.2 0.0 copy-start.2
  7.2 2.7 %route_body.1 = (bf16[128,3200]{1,0:T(8,128)(2,1)}, bf16[3,128,64]{2,1,0:T(8,128)(2,1)}) custom-call(s32[4,64]{1,0:T(4,128)} %bitcast.40, bf16[4,64]{1,0:T(4,128)(2,1)} %bitcast.41, bf16[64,1024]{1,0:T(8,128)(2,1)} %tok_hbm.1, bf16[64,1024]{1,0:T(8,128)(2,1)} %up_hbm.1), custom_call_target="tpu_custom_call" | custom-call | flops 80000000 | bytes 1300000 | tf_op jit(solution)/shard_map/route_body/pallas_call | solution.py:239
  9.9 15.2 %all-to-all-start = ((bf16[16,8,3200]{2,1,0:T(8,128)(2,1)}), bf16[16,8,3200]{2,1,0:T(8,128)(2,1)S(1)}, u32[]{:S(2)}, u32[]{:S(2)}) async-start(bf16[16,8,3200]{2,1,0:T(8,128)(2,1)} %bitcast.26), calls=%async_computation | async-start | bytes 1638400 | tf_op jit(solution)/shard_map/all_to_all | solution.py:252
  25.1 0.0 copy-done.2
  25.2 1.9 %collective-permute-start = (bf16[352,1024]{1,0:T(8,128)(2,1)S(1)}, bf16[352,1024]{1,0:T(8,128)(2,1)S(1)}, u32[]{:S(2)}, u32[]{:S(2)}) collective-permute-start(bf16[352,1024]{1,0:T(8,128)(2,1)S(1)} %bitcast.30), channel_id=1, source_target_pairs={{0,1},{1,0},{2,3},{3,2},{4,5},{5,4},{6,7},{7,6},{8,9},{9,8},{10,11... | collective-permute-start | bytes 2162696 | tf_op jit(solution)/shard_map/ppermute | solution.py:260
  27.1 0.0 copy-done.3
  27.1 2.4 %collective-permute-start.1 = (bf16[352,1024]{1,0:T(8,128)(2,1)S(1)}, bf16[352,1024]{1,0:T(8,128)(2,1)S(1)}, u32[]{:S(2)}, u32[]{:S(2)}) collective-permute-start(bf16[352,1024]{1,0:T(8,128)(2,1)S(1)} %bitcast.33), channel_id=1, source_target_pairs={{0,1},{1,0},{2,3},{3,2},{4,5},{5,4},{6,7},{7,6},{8,9},{9,8},{10,11... | collective-permute-start | bytes 2162696 | tf_op jit(solution)/shard_map/ppermute | solution.py:260
  29.5 1.9 %collective-permute-start.2 = (bf16[352,1024]{1,0:T(8,128)(2,1)}, bf16[352,1024]{1,0:T(8,128)(2,1)}, u32[]{:S(2)}, u32[]{:S(2)}) collective-permute-start(bf16[352,1024]{1,0:T(8,128)(2,1)} %bitcast.34), channel_id=1, source_target_pairs={{0,1},{1,0},{2,3},{3,2},{4,5},{5,4},{6,7},{7,6},{8,9},{9,8},{10,11... | collective-permute-start | bytes 2162696 | tf_op jit(solution)/shard_map/ppermute | solution.py:260
  31.4 0.0 collective-permute-done.refs_4_
  31.5 0.0 copy-start.4
  31.5 0.0 collective-permute-done.1.refs_5_
  31.5 0.8 copy-done.4
  32.3 0.9 copy-done.5
  33.2 0.8 collective-permute-done.2.refs_6_
  33.9 31.7 %all-to-all-done = bf16[16,8,3200]{2,1,0:T(8,128)(2,1)S(1)} async-done(((bf16[16,8,3200]{2,1,0:T(8,128)(2,1)}), bf16[16,8,3200]{2,1,0:T(8,128)(2,1)S(1)}, u32[]{:S(2)}, u32[]{:S(2)}) %all-to-all-start) | async-done | bytes 819232 | tf_op jit(solution)/shard_map/all_to_all | solution.py:252
  65.6 1.5 place_body.1
  67.2 16.9 %all_to_all.45 = bf16[4,80,2048]{2,1,0:T(8,128)(2,1)S(1)} all-to-all(bf16[4,80,2048]{2,1,0:T(8,128)(2,1)S(1)} %bitcast.17), channel_id=1, replica_groups={{0,2,4,6},{1,3,5,7},{8,10,12,14},{9,11,13,15},{16,18,20,22},{17,19,21,2..., dimensions={0} | all-to-all | bytes 2621440 | tf_op jit(solution)/shard_map/all_to_all | solution.py:256
  84.1 1.9 %collective-permute-start.3 = (bf16[320,2048]{1,0:T(8,128)(2,1)S(1)}, bf16[320,2048]{1,0:T(8,128)(2,1)S(1)}, u32[]{:S(2)}, u32[]{:S(2)}) collective-permute-start(bf16[320,2048]{1,0:T(8,128)(2,1)S(1)} %bitcast.23), channel_id=1, source_target_pairs={{0,1},{1,0},{2,3},{3,2},{4,5},{5,4},{6,7},{7,6},{8,9},{9,8},{10,11... | collective-permute-start | bytes 3932168 | tf_op jit(solution)/shard_map/ppermute | solution.py:260
  86.0 0.0 copy-done
  86.0 8.0 %own_body.1 = (bf16[320,1024]{1,0:T(8,128)(2,1)}, bf16[320,352]{1,0:T(8,128)(2,1)}, bf16[320,352]{1,0:T(8,128)(2,1)}, bf16[320,352]{1,0:T(8,128)(2,1)}) custom-call(bf16[320,2048]{1,0:T(8,128)(2,1)} %bitcast.24, bf16[352,1024]{1,0:T(8,128)(2,1)} %bitcast.28, bf16[352,1024]{1,0:T(8,128)(2,1)} %bitcast.31, bf16[352,1024]{1,0:T(8,128)(2,1)} %bitcast.35, ...), custom_call_target="tpu_custom_call" | custom-call | flops 2300000000 | bytes 7000000 | tf_op jit(solution)/shard_map/own_body/pallas_call | solution.py:239
  94.0 3.5 %all-to-all-start.2 = ((bf16[4,80,1024]{2,1,0:T(8,128)(2,1)}), bf16[4,80,1024]{2,1,0:T(8,128)(2,1)S(1)}, u32[]{:S(2)}, u32[]{:S(2)}) async-start(bf16[4,80,1024]{2,1,0:T(8,128)(2,1)} %bitcast.27), calls=%async_computation.3 | async-start | bytes 1310720 | tf_op jit(solution)/shard_map/all_to_all | solution.py:256
  97.5 0.0 reduce-scatter.2.cloned.1.call-start
  97.5 0.0 collective-permute-done.3.refs_0_
  97.5 0.0 copy-start.1
  97.6 1.1 copy-done.1
  98.7 6.9 %grads_body.1 = bf16[4,1056,256]{2,1,0:T(8,128)(2,1)} custom-call(bf16[320,2048]{1,0:T(8,128)(2,1)} %copy-done.1, bf16[352,1024]{1,0:T(8,128)(2,1)} %bitcast.29, bf16[352,1024]{1,0:T(8,128)(2,1)} %bitcast.32, bf16[352,1024]{1,0:T(8,128)(2,1)} %bitcast.36, bf16[320,2048]{1,0:T(8,128)(2,1)} %bitcast.25, bf16[320,352]{1,0:T(8,128)(2,1)} %get-tuple-element.34.refs_5_, ...), custom_call_target="tpu_custom_call" | custom-call | flops 2100000000 | bytes 8000000 | tf_op jit(solution)/shard_map/grads_body/pallas_call | solution.py:239
  105.6 0.0 reduce-scatter.2.cloned.1.call-update
  105.6 3.7 %all-to-all-done.2 = bf16[4,80,1024]{2,1,0:T(8,128)(2,1)S(1)} async-done(((bf16[4,80,1024]{2,1,0:T(8,128)(2,1)}), bf16[4,80,1024]{2,1,0:T(8,128)(2,1)S(1)}, u32[]{:S(2)}, u32[]{:S(2)}) %all-to-all-start.2) | async-done | bytes 655392 | tf_op jit(solution)/shard_map/all_to_all | solution.py:256
  109.3 0.5 node_body.1
  109.7 36.1 %all_to_all.46 = bf16[16,8,1536]{2,1,0:T(8,128)(2,1)} all-to-all(bf16[16,8,1536]{2,1,0:T(8,128)(2,1)S(1)} %bitcast.20), channel_id=1, replica_groups=mesh['dp'=4,'node'=16,'local'=8] {'node'}, dimensions={0} | all-to-all | bytes 786432 | tf_op jit(solution)/shard_map/all_to_all | solution.py:252
  145.8 2.2 %final_body.1 = (bf16[64,1024]{1,0:T(8,128)(2,1)}, bf16[352,256]{1,0:T(8,128)(2,1)}, bf16[352,256]{1,0:T(8,128)(2,1)}, bf16[352,256]{1,0:T(8,128)(2,1)}) custom-call(bf16[1056,256]{1,0:T(8,128)(2,1)} %reduce-scatter.2.cloned.1.call-done.sum_hbm, bf16[3,128,64]{2,1,0:T(8,128)(2,1)} %get-tuple-element.37.sel_hbm, bf16[128,1536]{1,0:T(8,128)(2,1)} %bitcast.22), custom_call_target="tpu_custom_call" | custom-call | flops 50000000 | bytes 1600000 | tf_op jit(solution)/shard_map/final_body/pallas_call | solution.py:239
  (3 shorter events, 0.0 us)
Async XLA Ops:
  7.2 19.9 %copy-start.3 = (bf16[1,352,1024]{2,1,0:T(8,128)(2,1)S(1)}, bf16[1,352,1024]{2,1,0:T(8,128)(2,1)}, u32[]{:S(2)}) copy-start(bf16[1,352,1024]{2,1,0:T(8,128)(2,1)} %param.12) | copy-start | bytes 2162692
  7.2 18.0 %copy-start.2 = (bf16[1,352,1024]{2,1,0:T(8,128)(2,1)S(1)}, bf16[1,352,1024]{2,1,0:T(8,128)(2,1)}, u32[]{:S(2)}) copy-start(bf16[1,352,1024]{2,1,0:T(8,128)(2,1)} %param.11) | copy-start | bytes 2162692
  9.9 55.7 %all-to-all-start = ((bf16[16,8,3200]{2,1,0:T(8,128)(2,1)}), bf16[16,8,3200]{2,1,0:T(8,128)(2,1)S(1)}, u32[]{:S(2)}, u32[]{:S(2)}) async-start(bf16[16,8,3200]{2,1,0:T(8,128)(2,1)} %bitcast.26), calls=%async_computation | async-start | bytes 1638400 | tf_op jit(solution)/shard_map/all_to_all | solution.py:252
  25.2 6.3 %collective-permute-start = (bf16[352,1024]{1,0:T(8,128)(2,1)S(1)}, bf16[352,1024]{1,0:T(8,128)(2,1)S(1)}, u32[]{:S(2)}, u32[]{:S(2)}) collective-permute-start(bf16[352,1024]{1,0:T(8,128)(2,1)S(1)} %bitcast.30), channel_id=1, source_target_pairs={{0,1},{1,0},{2,3},{3,2},{4,5},{5,4},{6,7},{7,6},{8,9},{9,8},{10,11... | collective-permute-start | bytes 2162696 | tf_op jit(solution)/shard_map/ppermute | solution.py:260
  27.1 4.4 %collective-permute-start.1 = (bf16[352,1024]{1,0:T(8,128)(2,1)S(1)}, bf16[352,1024]{1,0:T(8,128)(2,1)S(1)}, u32[]{:S(2)}, u32[]{:S(2)}) collective-permute-start(bf16[352,1024]{1,0:T(8,128)(2,1)S(1)} %bitcast.33), channel_id=1, source_target_pairs={{0,1},{1,0},{2,3},{3,2},{4,5},{5,4},{6,7},{7,6},{8,9},{9,8},{10,11... | collective-permute-start | bytes 2162696 | tf_op jit(solution)/shard_map/ppermute | solution.py:260
  29.5 4.4 %collective-permute-start.2 = (bf16[352,1024]{1,0:T(8,128)(2,1)}, bf16[352,1024]{1,0:T(8,128)(2,1)}, u32[]{:S(2)}, u32[]{:S(2)}) collective-permute-start(bf16[352,1024]{1,0:T(8,128)(2,1)} %bitcast.34), channel_id=1, source_target_pairs={{0,1},{1,0},{2,3},{3,2},{4,5},{5,4},{6,7},{7,6},{8,9},{9,8},{10,11... | collective-permute-start | bytes 2162696 | tf_op jit(solution)/shard_map/ppermute | solution.py:260
  31.5 0.9 copy-start.4
  32.3 0.9 copy-start.5
  84.1 1.9 %copy-start = (bf16[4,80,2048]{2,1,0:T(8,128)(2,1)}, bf16[4,80,2048]{2,1,0:T(8,128)(2,1)S(1)}, u32[]{:S(2)}) copy-start(bf16[4,80,2048]{2,1,0:T(8,128)(2,1)S(1)} %all_to_all.45) | copy-start | bytes 3932164
  84.1 13.5 %collective-permute-start.3 = (bf16[320,2048]{1,0:T(8,128)(2,1)S(1)}, bf16[320,2048]{1,0:T(8,128)(2,1)S(1)}, u32[]{:S(2)}, u32[]{:S(2)}) collective-permute-start(bf16[320,2048]{1,0:T(8,128)(2,1)S(1)} %bitcast.23), channel_id=1, source_target_pairs={{0,1},{1,0},{2,3},{3,2},{4,5},{5,4},{6,7},{7,6},{8,9},{9,8},{10,11... | collective-permute-start | bytes 3932168 | tf_op jit(solution)/shard_map/ppermute | solution.py:260
  94.0 15.3 %all-to-all-start.2 = ((bf16[4,80,1024]{2,1,0:T(8,128)(2,1)}), bf16[4,80,1024]{2,1,0:T(8,128)(2,1)S(1)}, u32[]{:S(2)}, u32[]{:S(2)}) async-start(bf16[4,80,1024]{2,1,0:T(8,128)(2,1)} %bitcast.27), calls=%async_computation.3 | async-start | bytes 1310720 | tf_op jit(solution)/shard_map/all_to_all | solution.py:256
  97.5 48.3 %reduce-scatter.2.cloned.1.call-start = ((), (), s32[]{:S(2)}) async-start(), calls=%async_computation.5 | async-start | bytes 2703360 | tf_op jit(solution)/shard_map/reduce_scatter | solution.py:337
  97.5 1.1 copy-start.1
Sparse Core Ops, SparseCore 0:
  105.7 38.1 reduce-scatter.1

commit v3 on v2

--- a/solution.py
+++ b/solution.py
@@ -132,71 +132,62 @@
     return act, up_value * sig * (1.0 + gate_logit * (1.0 - sig)), (act * up_value).astype(BF)
 
 
-def own_body(*refs):
-    hbm, (piece_hbm, bg_hbm, bu_hbm, hidden_hbm) = refs[0:7], refs[7:11]
-    vmem, (total_ref, piece_ref, bg_ref, bu_ref, hidden_ref, sems) = refs[11:18], refs[18:]
-    loads = [pltpu.make_async_copy(src, dst, sems.at[i]) for i, (src, dst) in enumerate(zip(hbm, vmem))]
-    for load in loads:
-        load.start()
-    backs = ((bg_ref, bg_hbm), (bu_ref, bu_hbm), (hidden_ref, hidden_hbm))
-    stores = [pltpu.make_async_copy(src, dst, sems.at[7 + i]) for i, (src, dst) in enumerate(backs)]
-    xc_ref = vmem[0]
-    loads[0].wait()
-    for half in range(2):
-        gate_ref, up_ref, down_ref = vmem[1 + 3 * half : 4 + 3 * half]
-        for load in loads[1 + 3 * half : 4 + 3 * half]:
-            load.wait()
-        for start in range(0, SENT, 160):
-            rows = pl.ds(start, 160)
-            x, c = xc_ref[rows, :WIDTH], xc_ref[rows, WIDTH:]
+def own_body(xc_ref, *refs):
+    own, rest, (piece_ref, back_ref) = refs[0:3], refs[3:6], refs[6:]
+    for start in range(0, SENT, 160):
+        rows = pl.ds(start, 160)
+        x, c = xc_ref[rows, :WIDTH], xc_ref[rows, WIDTH:]
+        total = None
+        for gate_ref, up_ref, down_ref in (own, rest):
             act, slope, hidden = activate(x, gate_ref, up_ref)
             back_hidden = mm_last(c, down_ref[...])
             back_up = (back_hidden * act).astype(BF)
             back_gate = (back_hidden * slope).astype(BF)
             part = mm(back_gate, gate_ref[...]) + mm(back_up, up_ref[...])
-            if half == 0:
-                bg_ref[rows] = back_gate
-                bu_ref[rows] = back_up
-                hidden_ref[rows] = hidden
-                total_ref[rows] = part
+            if total is None:
+                back_ref[0, rows] = back_gate
+                back_ref[1, rows] = back_up
+                back_ref[2, rows] = hidden
+                total = part
             else:
-                piece_ref[rows] = (total_ref[rows] + part).astype(BF)
-        if half == 0:
-            for store in stores:
-                store.start()
-    last = pltpu.make_async_copy(piece_ref, piece_hbm, sems.at[10])
-    last.start()
-    for store in stores:
-        store.wait()
-    last.wait()
+                total = total + part
+        piece_ref[rows] = total.astype(BF)
 
 
 def grads_body(*refs):
-    hbm, out_hbm, vmem, (out_ref, bg2_ref, bu2_ref, hidden2_ref, sems) = refs[0:8], refs[8], refs[9:17], refs[17:]
-    loads = [pltpu.make_async_copy(src, dst, sems.at[i]) for i, (src, dst) in enumerate(zip(hbm, vmem))]
-    for load in loads:
+    hbm, out_hbm, vmem, (out_ref, bg2_ref, bu2_ref, hidden2_ref, sems) = refs[0:6], refs[6:10], refs[10:16], refs[16:]
+    group = lax.axis_index("dp")
+    chunks = [pl.ds(0, 160), pl.ds(160, 160)]
+    rest_in = [pltpu.make_async_copy(hbm[0].at[r], vmem[0].at[r], sems.at[i]) for i, r in enumerate(chunks)]
+    loads = [pltpu.make_async_copy(hbm[i], vmem[i], sems.at[1 + i]) for i in range(1, 6)]
+    rest_ref, gate_ref, up_ref, down_ref, own_ref, back_ref = vmem
+    for load in (rest_in[0], loads[0], loads[1], loads[2], rest_in[1]):
         load.start()
-    rest_ref, gate_ref, up_ref, down_ref, own_ref, bg_ref, bu_ref, hidden_ref = vmem
-    for load in loads[:4]:
-        load.wait()
-    for start in range(0, SENT, 160):
-        rows = pl.ds(start, 160)
+    for chunk, rows in enumerate(chunks):
+        rest_in[chunk].wait()
+        if chunk == 0:
+            loads[0].wait()
+            loads[1].wait()
         act, slope, hidden2_ref[rows] = activate(rest_ref[rows, :WIDTH], gate_ref, up_ref)
+        if chunk == 0:
+            loads[2].wait()
+            loads[3].start()
+            loads[4].start()
         back_hidden = mm_last(rest_ref[rows, WIDTH:], down_ref[...])
         bu2_ref[rows] = (back_hidden * act).astype(BF)
         bg2_ref[rows] = (back_hidden * slope).astype(BF)
-    for load in loads[4:]:
-        load.wait()
-    parts = ((bg_ref, bg2_ref, 0), (bu_ref, bu2_ref, 0), (hidden_ref, hidden2_ref, WIDTH))
+    loads[3].wait()
+    loads[4].wait()
     stores = []
-    for kind, (lhs_own, lhs_rest, at) in enumerate(parts):
-        cols = pl.ds(at, WIDTH)
-        total = mm_first(lhs_own[...], own_ref[:, cols]) + mm_first(lhs_rest[...], rest_ref[:, cols])
-        rows = pl.ds(kind * HALF, HALF)
-        for d in range(4):
-            out_ref[d, rows] = total[:, d * 256 : (d + 1) * 256].astype(BF)
-        stores.append(pltpu.make_async_copy(out_ref.at[:, rows], out_hbm.at[:, rows], sems.at[8 + kind]))
-        stores[-1].start()
+    for kind, (lhs_rest, at) in enumerate(((bg2_ref, 0), (bu2_ref, 0), (hidden2_ref, WIDTH))):
+        cols, rows = pl.ds(at, WIDTH), pl.ds(kind * HALF, HALF)
+        total = mm_first(back_ref[kind], own_ref[:, cols]) + mm_first(lhs_rest[...], rest_ref[:, cols])
+        out_ref[rows] = total.astype(BF)
+        for shift in range(4):
+            target = pl.ds(pl.multiple_of(((group + shift) & 3) * 256, 256), 256)
+            copy = pltpu.make_async_copy(out_ref.at[rows, target], out_hbm[shift].at[rows], sems.at[7 + 4 * kind + shift])
+            stores.append(copy)
+            copy.start()
     for store in stores:
         store.wait()
 
@@ -209,36 +200,32 @@
     ).astype(BF)
 
 
-def final_body(sum_hbm, sel_hbm, msg_hbm, out_hbm, gate_hbm, up_hbm, down_hbm, sum_ref, sel_ref, msg_ref, out_ref, sems):
-    grads = []
-    for kind, grad_hbm in enumerate((gate_hbm, up_hbm, down_hbm)):
+def early_body(*refs):
+    total = refs[0][...].astype(F32)
+    for ref in refs[1:-1]:
+        total = total + ref[...].astype(F32)
+    refs[-1][...] = total
+
+
+def late_body(total_ref, *refs):
+    for kind, out_ref in enumerate(refs[-3:]):
         part = pl.ds(kind * HALF, HALF)
-        load = pltpu.make_async_copy(sum_hbm.at[part], sum_ref.at[part], sems.at[kind])
-        grads.append((load, pltpu.make_async_copy(sum_ref.at[part], grad_hbm, sems.at[3 + kind])))
-    loads = [pltpu.make_async_copy(sel_hbm, sel_ref, sems.at[6]), pltpu.make_async_copy(msg_hbm, msg_ref, sems.at[7])]
-    for load in loads:
-        load.start()
-    for load, _ in grads:
-        load.start()
-    for load, store in grads:
-        load.wait()
-        store.start()
-    for load in loads:
-        load.wait()
+        total = total_ref[part]
+        for ref in refs[:-3]:
+            total = total + ref[part].astype(F32)
+        out_ref[...] = total.astype(BF)
+
+
+def final_body(sel_ref, msg_ref, out_ref):
     low = msg_ref[:, WIDTH:]
     out_ref[:, :MID] = (mm_first(sel_ref[0], msg_ref[:, :MID]) + mm_first(sel_ref[1], low)).astype(BF)
     out_ref[:, MID:] = (mm_first(sel_ref[0], msg_ref[:, MID:WIDTH]) + mm_first(sel_ref[2], low)).astype(BF)
-    last = pltpu.make_async_copy(out_ref, out_hbm, sems.at[8])
-    last.start()
-    for _, store in grads:
-        store.wait()
-    last.wait()
-
-
-def call(body, ins, outs, flops, moved, *args, scratch=(), limit=60):
+
+
+def call(body, ins, outs, flops, moved, *args, scratch=(), limit=60, dtype=BF):
     return pl.pallas_call(
         body,
-        out_shape=tuple(jax.ShapeDtypeStruct(s, BF) for s, _ in outs),
+        out_shape=tuple(jax.ShapeDtypeStruct(s, dtype) for s, _ in outs),
         in_specs=list(ins),
         out_specs=tuple(m for _, m in outs),
         scratch_shapes=list(scratch),
@@ -254,6 +241,10 @@
 
 def over_chips(x):
     return lax.all_to_all(x, "local", split_axis=0, concat_axis=0, tiled=True, axis_index_groups=SAME_CORE)
+
+
+def next_group(x, shift):
+    return lax.ppermute(x, "dp", [(i, (i + shift) % 4) for i in range(4)])
 
 
 def other_core(x):
@@ -295,65 +286,70 @@
     )
     rows_own = over_chips(placed)
     rows_rest = other_core(rows_own)
-    piece, *back_own = call(
+    piece, back_own = call(
         own_body,
-        [HBM] * 7,
-        [((SENT, WIDTH), HBM)] + [((SENT, HALF), HBM)] * 3,
+        [VMEM] * 7,
+        [((SENT, WIDTH), VMEM), ((3, SENT, HALF), VMEM)],
         2_300_000_000,
         7_000_000,
         rows_own,
         *own,
         *rest,
-        scratch=[
-            pltpu.VMEM((SENT, 2 * WIDTH), BF),
-            *[pltpu.VMEM((HALF, WIDTH), BF)] * 6,
-            pltpu.VMEM((SENT, WIDTH), F32),
-            pltpu.VMEM((SENT, WIDTH), BF),
-            *[pltpu.VMEM((SENT, HALF), BF)] * 3,
-            pltpu.SemaphoreType.DMA((11,)),
-        ],
+        limit=24,
     )
     returned = over_chips(piece)
-    (grads,) = call(
+    grads = call(
         grads_body,
-        [HBM] * 8,
-        [((4, 3 * HALF, 256), HBM)],
+        [HBM] * 6,
+        [((3 * HALF, 256), HBM)] * 4,
         2_100_000_000,
         8_000_000,
         rows_rest,
         *own,
         rows_own,
-        *back_own,
+        back_own,
         scratch=[
             pltpu.VMEM((SENT, 2 * WIDTH), BF),
             *[pltpu.VMEM((HALF, WIDTH), BF)] * 3,
             pltpu.VMEM((SENT, 2 * WIDTH), BF),
+            pltpu.VMEM((3, SENT, HALF), BF),
+            pltpu.VMEM((3 * HALF, WIDTH), BF),
             *[pltpu.VMEM((SENT, HALF), BF)] * 3,
-            pltpu.VMEM((4, 3 * HALF, 256), BF),
-            *[pltpu.VMEM((SENT, HALF), BF)] * 3,
-            pltpu.SemaphoreType.DMA((11,)),
+            pltpu.SemaphoreType.DMA((19,)),
         ],
     )
-    summed = lax.psum_scatter(grads.reshape(12 * HALF, 256), "dp", scatter_dimension=0, tiled=True)
+    returned, *grads = lax.optimization_barrier((returned, *grads))
     (node_sum,) = call(node_body, [VMEM] * 2, [((MSG, WIDE), VMEM)], 50_000_000_000, 1_300_000, slot_sel, returned, limit=16)
-    token_grads, *weight_grads = call(
+    (partial,) = call(
+        early_body,
+        [VMEM] * 2,
+        [((3 * HALF, 256), VMEM)],
+        50_000_000_000,
+        2_700_000,
+        grads[0],
+        *(next_group(grads[shift], shift) for shift in (2,)),
+        dtype=F32,
+    )
+    totals = call(
+        late_body,
+        [VMEM] * 3,
+        [((HALF, 256), VMEM)] * 3,
+        1_000_000,
+        2_700_000,
+        partial,
+        *(next_group(grads[shift], shift) for shift in (1, 3)),
+    )
+    (token_grads,) = call(
         final_body,
-        [HBM] * 3,
-        [((TOKS, WIDTH), HBM)] + [((HALF, 256), HBM)] * 3,
+        [VMEM] * 2,
+        [((TOKS, WIDTH), VMEM)],
         50_000_000,
-        1_600_000,
-        summed,
+        700_000,
         row_sel,
         over_nodes(node_sum),
-        scratch=[
-            pltpu.VMEM((3 * HALF, 256), BF),
-            pltpu.VMEM((3, MSG, TOKS), BF),
-            pltpu.VMEM((MSG, WIDE), BF),
-            pltpu.VMEM((TOKS, WIDTH), BF),
-            pltpu.SemaphoreType.DMA((9,)),
-        ],
-    )
-    return (token_grads, *[g[None] for g in weight_grads])
+        limit=16,
+    )
+    return (token_grads, *[g[None] for g in totals])
 
 
 def solution(mesh):

time: 157 us -> 144 us (0.917)
  blocking collectives: 53 us -> 17 us
  starting transfers between devices: 26.9 us -> 48.8 us
  between operations: 14.2 us -> 0.95 us
  waiting for transfers between devices: 36.2 us -> 48.1 us
  Pallas kernels: 21.8 us -> 24 us
    all_to_all x1 -> x0, blocking collectives: 36.1 us -> none  [over_nodes(): return lax.all_to_all(x, 'node', split_axis=0, concat_axis=0, tiled=True)]
    all_to_all x1 -> x2, starting transfers between devices: 15.2 us -> 28 us  [over_nodes(): return lax.all_to_all(x, 'node', split_axis=0, concat_axis=0, tiled=True)]
    ppermute x0 -> x3, waiting for transfers between devices: none -> 11.1 us  [next_group(): return lax.ppermute(x, 'dp', [(i, (i + shift) % 4) for i in range(4)])]
    ppermute x0 -> x3, starting transfers between devices: none -> 9.15 us  [next_group(): return lax.ppermute(x, 'dp', [(i, (i + shift) % 4) for i in range(4)])]
    pallas_call x6 -> x8, Pallas kernels: 21.8 us -> 24 us  [call(): pl.pallas_call(body, out_shape=tuple((jax.ShapeDtypeStruct(s, dtype) for...]
    unnamed x12 -> x38, local copies, waits for them, and re-layouts: 2.82 us -> 4.27 us
    all_to_all x1 -> x2, waiting for transfers between devices: 31.7 us -> 31 us  [over_nodes(): return lax.all_to_all(x, 'node', split_axis=0, concat_axis=0, tiled=True)]
  transfers between devices with their start and end apart: 7 -> 10, of which waited for: 3 -> 5; matrix products, arithmetic and copies ran while one was open for 0% -> 0% of each run, Pallas kernels for 10% -> 13%
where the time goes in v3:
time: 144 us; the launch traced here: 143 us
  starting transfers between devices  48.8 us (34%)
  waiting for transfers between devices  48.1 us (33%)
  Pallas kernels  24 us (17%)
  blocking collectives  17 us (12%)
  local copies, waits for them, and re-layouts  4.27 us (3%)
    all_to_all x2, waiting for transfers between devices, over_nodes(): return lax.all_to_all(x, 'node', split_axis=0, concat_axis=0, tiled=True)  31 us
    all_to_all x2, starting transfers between devices, over_nodes(): return lax.all_to_all(x, 'node', split_axis=0, concat_axis=0, tiled=True)  28 us
    pallas_call x8, Pallas kernels, call(): pl.pallas_call(body, out_shape=tuple((jax.ShapeDtypeStruct(s, dtype) for...  24 us
    all_to_all x1, blocking collectives, over_chips(): lax.all_to_all(x, 'local', split_axis=0, concat_axis=0, tiled=True, axis_...  17 us
    ppermute x3, waiting for transfers between devices, next_group(): return lax.ppermute(x, 'dp', [(i, (i + shift) % 4) for i in range(4)])  11.1 us
    ppermute x3, starting transfers between devices, next_group(): return lax.ppermute(x, 'dp', [(i, (i + shift) % 4) for i in range(4)])  9.15 us
    ppermute x4, starting transfers between devices, other_core(): return lax.ppermute(x, 'local', OTHER_CORE)  8.16 us
    all_to_all x1, waiting for transfers between devices, over_chips(): lax.all_to_all(x, 'local', split_axis=0, concat_axis=0, tiled=True, axis_...  4.56 us
  transfers between devices with their start and end apart: 10, of which 5 were waited for; matrix products, arithmetic and copies ran while one was open for 0% of the time, Pallas kernels for 13%

profile of v3, /device:TPU:24, one launch (start us, length us, event | category | flops | bytes accessed | tf_op | source)
XLA Modules:
  0.0 143.1 jit_solution(10211405201937504193)
XLA Ops:
  0.6 0.0 copy-start.3
  0.6 0.0 copy-start.2
  0.7 2.7 %route_body.1 = (bf16[128,3200]{1,0:T(8,128)(2,1)}, bf16[3,128,64]{2,1,0:T(8,128)(2,1)}) custom-call(s32[4,64]{1,0:T(4,128)} %bitcast.36, bf16[4,64]{1,0:T(4,128)(2,1)} %bitcast.37, bf16[64,1024]{1,0:T(8,128)(2,1)} %tok_hbm.1, bf16[64,1024]{1,0:T(8,128)(2,1)} %up_hbm.1), custom_call_target="tpu_custom_call" | custom-call | flops 80000000 | bytes 1300000 | tf_op jit(solution)/shard_map/route_body/pallas_call | solution.py:226
  3.4 15.2 %all-to-all-start = ((bf16[16,8,3200]{2,1,0:T(8,128)(2,1)}), bf16[16,8,3200]{2,1,0:T(8,128)(2,1)S(1)}, u32[]{:S(2)}, u32[]{:S(2)}) async-start(bf16[16,8,3200]{2,1,0:T(8,128)(2,1)} %bitcast.32), calls=%async_computation | async-start | bytes 1638400 | tf_op jit(solution)/shard_map/all_to_all | solution.py:239
  18.6 1.9 %collective-permute-start = (bf16[352,1024]{1,0:T(8,128)(2,1)S(1)}, bf16[352,1024]{1,0:T(8,128)(2,1)S(1)}, u32[]{:S(2)}, u32[]{:S(2)}) collective-permute-start(bf16[352,1024]{1,0:T(8,128)(2,1)S(1)} %bitcast.24), channel_id=1, source_target_pairs={{0,1},{1,0},{2,3},{3,2},{4,5},{5,4},{6,7},{7,6},{8,9},{9,8},{10,11... | collective-permute-start | bytes 2162696 | tf_op jit(solution)/shard_map/ppermute | solution.py:251
  20.6 2.4 %collective-permute-start.1 = (bf16[352,1024]{1,0:T(8,128)(2,1)S(1)}, bf16[352,1024]{1,0:T(8,128)(2,1)S(1)}, u32[]{:S(2)}, u32[]{:S(2)}) collective-permute-start(bf16[352,1024]{1,0:T(8,128)(2,1)S(1)} %bitcast.27), channel_id=1, source_target_pairs={{0,1},{1,0},{2,3},{3,2},{4,5},{5,4},{6,7},{7,6},{8,9},{9,8},{10,11... | collective-permute-start | bytes 2162696 | tf_op jit(solution)/shard_map/ppermute | solution.py:251
  23.0 1.9 %collective-permute-start.2 = (bf16[352,1024]{1,0:T(8,128)(2,1)}, bf16[352,1024]{1,0:T(8,128)(2,1)S(1)}, u32[]{:S(2)}, u32[]{:S(2)}) collective-permute-start(bf16[352,1024]{1,0:T(8,128)(2,1)} %bitcast.29), channel_id=1, source_target_pairs={{0,1},{1,0},{2,3},{3,2},{4,5},{5,4},{6,7},{7,6},{8,9},{9,8},{10,11... | collective-permute-start | bytes 2162696 | tf_op jit(solution)/shard_map/ppermute | solution.py:251
  24.9 0.9 copy-done.7
  25.8 1.4 %collective-permute-done.2.refs_5_ = bf16[352,1024]{1,0:T(8,128)(2,1)S(1)} collective-permute-done((bf16[352,1024]{1,0:T(8,128)(2,1)}, bf16[352,1024]{1,0:T(8,128)(2,1)S(1)}, u32[]{:S(2)}, u32[]{:S(2)}) %collective-permute-start.2) | collective-permute-done | bytes 720928 | tf_op jit(solution)/shard_map/ppermute | solution.py:251
  27.3 0.9 copy-done.9
  28.1 31.0 %all-to-all-done = bf16[16,8,3200]{2,1,0:T(8,128)(2,1)S(1)} async-done(((bf16[16,8,3200]{2,1,0:T(8,128)(2,1)}), bf16[16,8,3200]{2,1,0:T(8,128)(2,1)S(1)}, u32[]{:S(2)}, u32[]{:S(2)}) %all-to-all-start) | async-done | bytes 819232 | tf_op jit(solution)/shard_map/all_to_all | solution.py:239
  59.1 1.5 %place_body.1 = (bf16[320,2048]{1,0:T(8,128)(2,1)S(1)}, bf16[320,384]{1,0:T(8,128)(2,1)S(1)}) custom-call(bf16[128,3200]{1,0:T(8,128)(2,1)S(1)} %bitcast.21), custom_call_target="tpu_custom_call" | custom-call | flops 400000000 | bytes 2300000 | tf_op jit(solution)/shard_map/place_body/pallas_call | solution.py:226
  60.7 0.0 copy-start.4
  60.7 17.0 %all_to_all.46 = bf16[4,80,2048]{2,1,0:T(8,128)(2,1)S(1)} all-to-all(bf16[4,80,2048]{2,1,0:T(8,128)(2,1)S(1)} %bitcast.20), channel_id=1, replica_groups={{0,2,4,6},{1,3,5,7},{8,10,12,14},{9,11,13,15},{16,18,20,22},{17,19,21,2..., dimensions={0} | all-to-all | bytes 2621440 | tf_op jit(solution)/shard_map/all_to_all | solution.py:243
  77.7 1.9 %collective-permute-start.3 = (bf16[320,2048]{1,0:T(8,128)(2,1)S(1)}, bf16[320,2048]{1,0:T(8,128)(2,1)}, u32[]{:S(2)}, u32[]{:S(2)}) collective-permute-start(bf16[320,2048]{1,0:T(8,128)(2,1)S(1)} %bitcast.17), channel_id=1, source_target_pairs={{0,1},{1,0},{2,3},{3,2},{4,5},{5,4},{6,7},{7,6},{8,9},{9,8},{10,11... | collective-permute-start | bytes 3932168 | tf_op jit(solution)/shard_map/ppermute | solution.py:251
  79.7 5.7 %own_body.1 = (bf16[320,1024]{1,0:T(8,128)(2,1)}, bf16[3,320,352]{2,1,0:T(8,128)(2,1)S(1)}) custom-call(bf16[320,2048]{1,0:T(8,128)(2,1)S(1)} %bitcast.18, bf16[352,1024]{1,0:T(8,128)(2,1)S(1)} %bitcast.25, bf16[352,1024]{1,0:T(8,128)(2,1)S(1)} %bitcast.28, bf16[352,1024]{1,0:T(8,128)(2,1)S(1)} %bitcast.31, bf16[352,1024]{1,0:T(8,128)(2,1)S(1)} %copy-done.6, ...), custom_call_target="tpu_custom_call" | custom-call | flops 2300000000 | bytes 7000000 | tf_op jit(solution)/shard_map/own_body/pallas_call | solution.py:226
  85.4 0.9 copy-done.13
  86.2 3.5 %all-to-all-start.2 = ((bf16[4,80,1024]{2,1,0:T(8,128)(2,1)}), bf16[4,80,1024]{2,1,0:T(8,128)(2,1)S(1)}, u32[]{:S(2)}, u32[]{:S(2)}) async-start(bf16[4,80,1024]{2,1,0:T(8,128)(2,1)} %bitcast.9), calls=%async_computation.2 | async-start | bytes 1310720 | tf_op jit(solution)/shard_map/all_to_all | solution.py:243
  89.8 7.2 %grads_body.1 = (bf16[1056,256]{1,0:T(8,128)(2,1)}, bf16[1056,256]{1,0:T(8,128)(2,1)}, bf16[1056,256]{1,0:T(8,128)(2,1)}, bf16[1056,256]{1,0:T(8,128)(2,1)}) custom-call(bf16[320,2048]{1,0:T(8,128)(2,1)} %collective-permute-done.3.refs_0_, bf16[352,1024]{1,0:T(8,128)(2,1)} %bitcast.23, bf16[352,1024]{1,0:T(8,128)(2,1)} %bitcast.26, ...), custom_call_target="tpu_custom_call" | custom-call | flops 2100000000 | bytes 8000000 | tf_op jit(solution)/shard_map/grads_body/pallas_call | solution.py:226
  97.0 4.6 %all-to-all-done.2 = bf16[4,80,1024]{2,1,0:T(8,128)(2,1)S(1)} async-done(((bf16[4,80,1024]{2,1,0:T(8,128)(2,1)}), bf16[4,80,1024]{2,1,0:T(8,128)(2,1)S(1)}, u32[]{:S(2)}, u32[]{:S(2)}) %all-to-all-start.2) | async-done | bytes 655392 | tf_op jit(solution)/shard_map/all_to_all | solution.py:243
  101.5 3.1 %collective-permute-start.4 = (bf16[1056,256]{1,0:T(8,128)(2,1)}, bf16[1056,256]{1,0:T(8,128)(2,1)S(1)}, u32[]{:S(2)}, u32[]{:S(2)}) collective-permute-start(bf16[1056,256]{1,0:T(8,128)(2,1)} %get-tuple-element.50), channel_id=1, source_target_pairs={{0,256},{128,384},{256,0},{384,128},{1,257},{129,385},{257,1},{385... | collective-permute-start | bytes 1622024 | tf_op jit(solution)/shard_map/ppermute | solution.py:247
  104.7 1.2 node_body.1
  105.9 12.8 %all-to-all-start.3 = ((bf16[16,8,1536]{2,1,0:T(8,128)(2,1)}), bf16[16,8,1536]{2,1,0:T(8,128)(2,1)S(1)}, u32[]{:S(2)}, u32[]{:S(2)}) async-start(bf16[16,8,1536]{2,1,0:T(8,128)(2,1)} %bitcast.11), calls=%async_computation.3 | async-start | bytes 786432 | tf_op jit(solution)/shard_map/all_to_all | solution.py:239
  118.7 4.1 %collective-permute-start.5 = (bf16[1056,256]{1,0:T(8,128)(2,1)S(1)}, bf16[1056,256]{1,0:T(8,128)(2,1)S(1)}, u32[]{:S(2)}, u32[]{:S(2)}) collective-permute-start(bf16[1056,256]{1,0:T(8,128)(2,1)S(1)} %copy-done.17), channel_id=1, source_target_pairs={{0,128},{128,256},{256,384},{384,0},{1,129},{129,257},{257,385},{3... | collective-permute-start | bytes 1622024 | tf_op jit(solution)/shard_map/ppermute | solution.py:247
  122.9 1.9 %collective-permute-start.6 = (bf16[1056,256]{1,0:T(8,128)(2,1)S(1)}, bf16[1056,256]{1,0:T(8,128)(2,1)S(1)}, u32[]{:S(2)}, u32[]{:S(2)}) collective-permute-start(bf16[1056,256]{1,0:T(8,128)(2,1)S(1)} %copy-done.16), channel_id=1, source_target_pairs={{0,384},{128,0},{256,128},{384,256},{1,385},{129,1},{257,129},{385... | collective-permute-start | bytes 1622024 | tf_op jit(solution)/shard_map/ppermute | solution.py:247
  124.8 0.8 copy-done.18
  125.6 2.3 %early_body.1.total_ref = f32[1056,256]{1,0:T(8,128)} custom-call(bf16[1056,256]{1,0:T(8,128)(2,1)} %get-tuple-element.49.refs_0_, bf16[1056,256]{1,0:T(8,128)(2,1)} %copy-done.18), custom_call_target="tpu_custom_call" | custom-call | flops 49999998976 | bytes 2700000 | tf_op jit(solution)/shard_map/early_body/pallas_call | solution.py:226
  127.9 6.1 %collective-permute-done.5.refs_0_ = bf16[1056,256]{1,0:T(8,128)(2,1)S(1)} collective-permute-done((bf16[1056,256]{1,0:T(8,128)(2,1)S(1)}, bf16[1056,256]{1,0:T(8,128)(2,1)S(1)}, u32[]{:S(2)}, u32[]{:S(2)}) %collective-permute-start.5) | collective-permute-done | bytes 540704 | tf_op jit(solution)/shard_map/ppermute | solution.py:247
  134.0 5.0 %collective-permute-done.6.refs_1_ = bf16[1056,256]{1,0:T(8,128)(2,1)S(1)} collective-permute-done((bf16[1056,256]{1,0:T(8,128)(2,1)S(1)}, bf16[1056,256]{1,0:T(8,128)(2,1)S(1)}, u32[]{:S(2)}, u32[]{:S(2)}) %collective-permute-start.6) | collective-permute-done | bytes 540704 | tf_op jit(solution)/shard_map/ppermute | solution.py:247
  139.0 0.8 copy-done.15
  139.8 2.4 %late_body.1 = (bf16[352,256]{1,0:T(8,128)(2,1)}, bf16[352,256]{1,0:T(8,128)(2,1)}, bf16[352,256]{1,0:T(8,128)(2,1)}) custom-call(f32[1056,256]{1,0:T(8,128)} %early_body.1.total_ref, bf16[1056,256]{1,0:T(8,128)(2,1)} %copy-done.14, bf16[1056,256]{1,0:T(8,128)(2,1)} %copy-done.15), custom_call_target="tpu_custom_call" | custom-call | flops 1000000 | bytes 2700000 | tf_op jit(solution)/shard_map/late_body/pallas_call | solution.py:226
  142.2 0.9 final_body.1
  (35 shorter events, 0.1 us)
Async XLA Ops:
  0.6 19.9 %copy-start.3 = (bf16[1,352,1024]{2,1,0:T(8,128)(2,1)S(1)}, bf16[1,352,1024]{2,1,0:T(8,128)(2,1)}, u32[]{:S(2)}) copy-start(bf16[1,352,1024]{2,1,0:T(8,128)(2,1)} %param.12) | copy-start | bytes 2162692
  0.6 18.0 %copy-start.2 = (bf16[1,352,1024]{2,1,0:T(8,128)(2,1)S(1)}, bf16[1,352,1024]{2,1,0:T(8,128)(2,1)}, u32[]{:S(2)}) copy-start(bf16[1,352,1024]{2,1,0:T(8,128)(2,1)} %param.11) | copy-start | bytes 2162692
  3.4 55.7 %all-to-all-start = ((bf16[16,8,3200]{2,1,0:T(8,128)(2,1)}), bf16[16,8,3200]{2,1,0:T(8,128)(2,1)S(1)}, u32[]{:S(2)}, u32[]{:S(2)}) async-start(bf16[16,8,3200]{2,1,0:T(8,128)(2,1)} %bitcast.32), calls=%async_computation | async-start | bytes 1638400 | tf_op jit(solution)/shard_map/all_to_all | solution.py:239
  18.6 6.3 %collective-permute-start = (bf16[352,1024]{1,0:T(8,128)(2,1)S(1)}, bf16[352,1024]{1,0:T(8,128)(2,1)S(1)}, u32[]{:S(2)}, u32[]{:S(2)}) collective-permute-start(bf16[352,1024]{1,0:T(8,128)(2,1)S(1)} %bitcast.24), channel_id=1, source_target_pairs={{0,1},{1,0},{2,3},{3,2},{4,5},{5,4},{6,7},{7,6},{8,9},{9,8},{10,11... | collective-permute-start | bytes 2162696 | tf_op jit(solution)/shard_map/ppermute | solution.py:251
  20.6 4.4 %collective-permute-start.1 = (bf16[352,1024]{1,0:T(8,128)(2,1)S(1)}, bf16[352,1024]{1,0:T(8,128)(2,1)S(1)}, u32[]{:S(2)}, u32[]{:S(2)}) collective-permute-start(bf16[352,1024]{1,0:T(8,128)(2,1)S(1)} %bitcast.27), channel_id=1, source_target_pairs={{0,1},{1,0},{2,3},{3,2},{4,5},{5,4},{6,7},{7,6},{8,9},{9,8},{10,11... | collective-permute-start | bytes 2162696 | tf_op jit(solution)/shard_map/ppermute | solution.py:251
  23.0 4.3 %collective-permute-start.2 = (bf16[352,1024]{1,0:T(8,128)(2,1)}, bf16[352,1024]{1,0:T(8,128)(2,1)S(1)}, u32[]{:S(2)}, u32[]{:S(2)}) collective-permute-start(bf16[352,1024]{1,0:T(8,128)(2,1)} %bitcast.29), channel_id=1, source_target_pairs={{0,1},{1,0},{2,3},{3,2},{4,5},{5,4},{6,7},{7,6},{8,9},{9,8},{10,11... | collective-permute-start | bytes 2162696 | tf_op jit(solution)/shard_map/ppermute | solution.py:251
  24.9 35.7 %copy-start.5 = (bf16[352,1024]{1,0:T(8,128)(2,1)}, bf16[352,1024]{1,0:T(8,128)(2,1)S(1)}, u32[]{:S(2)}) copy-start(bf16[352,1024]{1,0:T(8,128)(2,1)S(1)} %collective-permute-done.refs_3_) | copy-start | bytes 2162692
  24.9 0.9 copy-start.7
  27.3 0.9 copy-start.9
  59.1 20.5 %copy-start.10 = (bf16[352,1024]{1,0:T(8,128)(2,1)S(1)}, bf16[352,1024]{1,0:T(8,128)(2,1)}, u32[]{:S(2)}) copy-start(bf16[352,1024]{1,0:T(8,128)(2,1)} %copy-done.9) | copy-start | bytes 2162692
  60.6 17.1 %copy-start.11 = (bf16[320,384]{1,0:T(8,128)(2,1)}, bf16[320,384]{1,0:T(8,128)(2,1)S(1)}, u32[]{:S(2)}) copy-start(bf16[320,384]{1,0:T(8,128)(2,1)S(1)} %get-tuple-element.37.sel_ref) | copy-start | bytes 737284
  60.7 19.0 %copy-start.4 = (bf16[1,352,1024]{2,1,0:T(8,128)(2,1)S(1)}, bf16[1,352,1024]{2,1,0:T(8,128)(2,1)}, u32[]{:S(2)}) copy-start(bf16[1,352,1024]{2,1,0:T(8,128)(2,1)} %param.13) | copy-start | bytes 2162692
  60.7 19.0 %copy-start.6 = (bf16[352,1024]{1,0:T(8,128)(2,1)S(1)}, bf16[352,1024]{1,0:T(8,128)(2,1)}, u32[]{:S(2)}) copy-start(bf16[352,1024]{1,0:T(8,128)(2,1)} %copy-done.5) | copy-start | bytes 2162692
  60.7 19.0 %copy-start.8 = (bf16[352,1024]{1,0:T(8,128)(2,1)S(1)}, bf16[352,1024]{1,0:T(8,128)(2,1)}, u32[]{:S(2)}) copy-start(bf16[352,1024]{1,0:T(8,128)(2,1)} %copy-done.7) | copy-start | bytes 2162692
  77.7 7.7 %copy-start = (bf16[4,80,2048]{2,1,0:T(8,128)(2,1)}, bf16[4,80,2048]{2,1,0:T(8,128)(2,1)S(1)}, u32[]{:S(2)}) copy-start(bf16[4,80,2048]{2,1,0:T(8,128)(2,1)S(1)} %all_to_all.46) | copy-start | bytes 3932164
  77.7 12.0 %collective-permute-start.3 = (bf16[320,2048]{1,0:T(8,128)(2,1)S(1)}, bf16[320,2048]{1,0:T(8,128)(2,1)}, u32[]{:S(2)}, u32[]{:S(2)}) collective-permute-start(bf16[320,2048]{1,0:T(8,128)(2,1)S(1)} %bitcast.17), channel_id=1, source_target_pairs={{0,1},{1,0},{2,3},{3,2},{4,5},{5,4},{6,7},{7,6},{8,9},{9,8},{10,11... | collective-permute-start | bytes 3932168 | tf_op jit(solution)/shard_map/ppermute | solution.py:251
  85.4 0.9 copy-start.13
  86.2 15.3 %all-to-all-start.2 = ((bf16[4,80,1024]{2,1,0:T(8,128)(2,1)}), bf16[4,80,1024]{2,1,0:T(8,128)(2,1)S(1)}, u32[]{:S(2)}, u32[]{:S(2)}) async-start(bf16[4,80,1024]{2,1,0:T(8,128)(2,1)} %bitcast.9), calls=%async_computation.2 | async-start | bytes 1310720 | tf_op jit(solution)/shard_map/all_to_all | solution.py:243
  89.7 14.9 %copy-start.12 = (bf16[320,384]{1,0:T(8,128)(2,1)S(1)}, bf16[320,384]{1,0:T(8,128)(2,1)}, u32[]{:S(2)}) copy-start(bf16[320,384]{1,0:T(8,128)(2,1)} %copy-done.11) | copy-start | bytes 737284
  101.5 23.3 %collective-permute-start.4 = (bf16[1056,256]{1,0:T(8,128)(2,1)}, bf16[1056,256]{1,0:T(8,128)(2,1)S(1)}, u32[]{:S(2)}, u32[]{:S(2)}) collective-permute-start(bf16[1056,256]{1,0:T(8,128)(2,1)} %get-tuple-element.50), channel_id=1, source_target_pairs={{0,256},{128,384},{256,0},{384,128},{1,257},{129,385},{257,1},{385... | collective-permute-start | bytes 1622024 | tf_op jit(solution)/shard_map/ppermute | solution.py:247
  104.7 14.1 %copy-start.17 = (bf16[1056,256]{1,0:T(8,128)(2,1)S(1)}, bf16[1056,256]{1,0:T(8,128)(2,1)}, u32[]{:S(2)}) copy-start(bf16[1056,256]{1,0:T(8,128)(2,1)} %get-tuple-element.51) | copy-start | bytes 1622020
  104.7 18.2 %copy-start.16 = (bf16[1056,256]{1,0:T(8,128)(2,1)S(1)}, bf16[1056,256]{1,0:T(8,128)(2,1)}, u32[]{:S(2)}) copy-start(bf16[1056,256]{1,0:T(8,128)(2,1)} %get-tuple-element.52) | copy-start | bytes 1622020
  105.9 36.3 %all-to-all-start.3 = ((bf16[16,8,1536]{2,1,0:T(8,128)(2,1)}), bf16[16,8,1536]{2,1,0:T(8,128)(2,1)S(1)}, u32[]{:S(2)}, u32[]{:S(2)}) async-start(bf16[16,8,1536]{2,1,0:T(8,128)(2,1)} %bitcast.11), calls=%async_computation.3 | async-start | bytes 786432 | tf_op jit(solution)/shard_map/all_to_all | solution.py:239
  118.7 15.2 %collective-permute-start.5 = (bf16[1056,256]{1,0:T(8,128)(2,1)S(1)}, bf16[1056,256]{1,0:T(8,128)(2,1)S(1)}, u32[]{:S(2)}, u32[]{:S(2)}) collective-permute-start(bf16[1056,256]{1,0:T(8,128)(2,1)S(1)} %copy-done.17), channel_id=1, source_target_pairs={{0,128},{128,256},{256,384},{384,0},{1,129},{129,257},{257,385},{3... | collective-permute-start | bytes 1622024 | tf_op jit(solution)/shard_map/ppermute | solution.py:247
  122.9 16.2 %collective-permute-start.6 = (bf16[1056,256]{1,0:T(8,128)(2,1)S(1)}, bf16[1056,256]{1,0:T(8,128)(2,1)S(1)}, u32[]{:S(2)}, u32[]{:S(2)}) collective-permute-start(bf16[1056,256]{1,0:T(8,128)(2,1)S(1)} %copy-done.16), channel_id=1, source_target_pairs={{0,384},{128,0},{256,128},{384,256},{1,385},{129,1},{257,129},{385... | collective-permute-start | bytes 1622024 | tf_op jit(solution)/shard_map/ppermute | solution.py:247
  124.8 0.8 copy-start.18
  127.9 14.3 %copy-start.1 = (bf16[3,128,64]{2,1,0:T(8,128)(2,1)S(1)}, bf16[3,128,64]{2,1,0:T(8,128)(2,1)}, u32[]{:S(2)}) copy-start(bf16[3,128,64]{2,1,0:T(8,128)(2,1)} %get-tuple-element.30.sel_ref) | copy-start | bytes 147460
  134.0 5.1 %copy-start.14 = (bf16[1056,256]{1,0:T(8,128)(2,1)}, bf16[1056,256]{1,0:T(8,128)(2,1)S(1)}, u32[]{:S(2)}) copy-start(bf16[1056,256]{1,0:T(8,128)(2,1)S(1)} %collective-permute-done.5.refs_0_) | copy-start | bytes 1622020
  139.0 0.8 copy-start.15

commit v4 on v3

--- a/solution.py
+++ b/solution.py
@@ -13,6 +13,7 @@
 TOKS = 64
 MSG = 128
 CAP = 5
+STEP = 320
 SLOT = 80
 SENT = 320
 F32 = jnp.float32
@@ -43,7 +44,7 @@
     return jnp.where(cond, 1.0, 0.0).astype(BF)
 
 
-def route_body(ids_hbm, gate_hbm, tok_hbm, up_hbm, msg_ref, sel_hbm, ids_ref, gate_ref, tok_ref, up_ref, sel_ref, sems):
+def route_body(ids_hbm, gate_hbm, tok_hbm, up_hbm, msg_hbm, sel_hbm, ids_ref, gate_ref, tok_ref, up_ref, msg_ref, sel_ref, sems):
     pairs = ((ids_hbm, ids_ref), (gate_hbm, gate_ref), (tok_hbm, tok_ref), (up_hbm, up_ref))
     loads = [pltpu.make_async_copy(src, dst, sems.at[i]) for i, (src, dst) in enumerate(pairs)]
     for load in loads:
@@ -71,8 +72,8 @@
     sel_ref[0] = whole
     sel_ref[1] = left
     sel_ref[2] = right
-    store = pltpu.make_async_copy(sel_ref, sel_hbm, sems.at[4])
-    store.start()
+    stores = [pltpu.make_async_copy(sel_ref, sel_hbm, sems.at[4])]
+    stores[0].start()
     own_node = (iota((MSG, TOKS), 1) >> 2) == node
     gate_whole = jnp.where(own_node, mm_last(whole, weight), 0.0).astype(BF)
     gate_late = jnp.where(own_node, mm_last(left + right, weight), 0.0).astype(BF)
@@ -84,7 +85,11 @@
         msg_ref[:, base : base + WIDTH] = mm(whole, src[...]).astype(BF)
         low = mm(left, src[:, :MID]) + mm(right, src[:, MID:])
         msg_ref[:, base + WIDTH : base + WIDE] = low.astype(BF)
-    store.wait()
+        part = pl.ds(base, WIDE + base // 12)
+        stores.append(pltpu.make_async_copy(msg_ref.at[:, part], msg_hbm.at[:, part], sems.at[5 + len(stores)]))
+        stores[-1].start()
+    for store in stores:
+        store.wait()
 
 
 def spread(sel, msg_ref, at, out_ref, to):
@@ -95,7 +100,15 @@
     out_ref[:, to + MID : to + WIDTH] = right.astype(BF)
 
 
-def place_body(msg_ref, out_ref, sel_hbm, sel_ref, gated_ref, sem):
+def fill(slot, sel_ref, part, gate=None):
+    slots = iota((SLOT, MSG), 0).astype(slot.dtype)
+    for j in range(4):
+        value = 1.0 if gate is None else gate[j : j + 1]
+        match = jnp.where(slots == slot[j : j + 1], value, 0.0)
+        sel_ref[pl.ds(j * SLOT, SLOT), pl.ds(part * MSG, MSG)] = match.astype(BF)
+
+
+def place_body(msg_ref, out_ref, slot_ref, sel_ref, gated_ref):
     row, col = iota((MSG, MSG), 0), iota((MSG, MSG), 1)
     gates = mm_first(msg_ref[:, META:], one(row == col))
     gate_whole, gate_late = gates[0:8], gates[8:16]
@@ -109,19 +122,12 @@
     slot_late = jnp.where(gate_late > 0.0, node + rank_late.astype(jnp.int32), -1)
     slot_left = jnp.where(lane_place < 4, slot_late, -1)
     slot_right = jnp.where(lane_place >= 4, slot_late, -1)
-    slots = iota((SLOT, MSG), 0)
-    for j in range(4):
-        parts = ((slot_whole, gate_whole), (slot_left, gate_late), (slot_right, gate_late))
-        for part, (slot, gate) in enumerate(parts):
-            match = slots == slot[j : j + 1]
-            rows, lanes = pl.ds(j * SLOT, SLOT), pl.ds(part * MSG, MSG)
-            sel_ref[rows, lanes] = one(match)
-            gated_ref[rows, lanes] = jnp.where(match, gate[j : j + 1], 0.0).astype(BF)
-    store = pltpu.make_async_copy(sel_ref, sel_hbm, sem)
-    store.start()
+    for part, (slot, gate) in enumerate(((slot_whole, gate_whole), (slot_left, gate_late), (slot_right, gate_late))):
+        slot_ref[16 * part : 16 * part + 16] = jnp.concatenate([slot, slot], 0).astype(F32).astype(BF)
+        fill(slot, sel_ref, part)
+        fill(slot, gated_ref, part, gate)
     spread(sel_ref, msg_ref, 0, out_ref, 0)
     spread(gated_ref, msg_ref, WIDE, out_ref, WIDTH)
-    store.wait()
 
 
 def activate(x, gate_ref, up_ref):
@@ -133,66 +139,61 @@
 
 
 def own_body(xc_ref, *refs):
-    own, rest, (piece_ref, back_ref) = refs[0:3], refs[3:6], refs[6:]
-    for start in range(0, SENT, 160):
-        rows = pl.ds(start, 160)
+    own, rest, piece_ref = refs[0:3], refs[3:6], refs[6]
+    for start in range(0, SENT, STEP):
+        rows = pl.ds(start, STEP)
         x, c = xc_ref[rows, :WIDTH], xc_ref[rows, WIDTH:]
         total = None
         for gate_ref, up_ref, down_ref in (own, rest):
-            act, slope, hidden = activate(x, gate_ref, up_ref)
+            act, slope, _ = activate(x, gate_ref, up_ref)
             back_hidden = mm_last(c, down_ref[...])
             back_up = (back_hidden * act).astype(BF)
             back_gate = (back_hidden * slope).astype(BF)
             part = mm(back_gate, gate_ref[...]) + mm(back_up, up_ref[...])
-            if total is None:
-                back_ref[0, rows] = back_gate
-                back_ref[1, rows] = back_up
-                back_ref[2, rows] = hidden
-                total = part
-            else:
-                total = total + part
+            total = part if total is None else total + part
         piece_ref[rows] = total.astype(BF)
 
 
 def grads_body(*refs):
-    hbm, out_hbm, vmem, (out_ref, bg2_ref, bu2_ref, hidden2_ref, sems) = refs[0:6], refs[6:10], refs[10:16], refs[16:]
+    hbm, out_hbm, vmem, (out_ref, sems) = refs[0:5], refs[5:9], refs[9:14], refs[14:]
     group = lax.axis_index("dp")
-    chunks = [pl.ds(0, 160), pl.ds(160, 160)]
-    rest_in = [pltpu.make_async_copy(hbm[0].at[r], vmem[0].at[r], sems.at[i]) for i, r in enumerate(chunks)]
-    loads = [pltpu.make_async_copy(hbm[i], vmem[i], sems.at[1 + i]) for i in range(1, 6)]
-    rest_ref, gate_ref, up_ref, down_ref, own_ref, back_ref = vmem
-    for load in (rest_in[0], loads[0], loads[1], loads[2], rest_in[1]):
+    own_ref, gate_ref, up_ref, down_ref, rest_ref = vmem
+    loads = [pltpu.make_async_copy(src, dst, sems.at[i]) for i, (src, dst) in enumerate(zip(hbm, vmem))]
+    for load in loads[:4]:
         load.start()
-    for chunk, rows in enumerate(chunks):
-        rest_in[chunk].wait()
-        if chunk == 0:
-            loads[0].wait()
-            loads[1].wait()
-        act, slope, hidden2_ref[rows] = activate(rest_ref[rows, :WIDTH], gate_ref, up_ref)
-        if chunk == 0:
-            loads[2].wait()
-            loads[3].start()
-            loads[4].start()
-        back_hidden = mm_last(rest_ref[rows, WIDTH:], down_ref[...])
-        bu2_ref[rows] = (back_hidden * act).astype(BF)
-        bg2_ref[rows] = (back_hidden * slope).astype(BF)
-    loads[3].wait()
-    loads[4].wait()
+    for load in loads[:3]:
+        load.wait()
+    loads[4].start()
+    backs = []
+    for rows_ref, ready in ((own_ref, loads[3]), (rest_ref, loads[4])):
+        if rows_ref is rest_ref:
+            ready.wait()
+        x = rows_ref[:, :WIDTH]
+        gate_logit, up_value = mm_last(gate_ref[...], x), mm_last(up_ref[...], x)
+        sig = jax.nn.sigmoid(gate_logit)
+        act = gate_logit * sig
+        if rows_ref is own_ref:
+            ready.wait()
+        back_hidden = mm_last(down_ref[...], rows_ref[:, WIDTH:])
+        slope = up_value * sig * (1.0 + gate_logit * (1.0 - sig))
+        backs.append([(back_hidden * slope).astype(BF), (back_hidden * act).astype(BF), (act * up_value).astype(BF)])
     stores = []
-    for kind, (lhs_rest, at) in enumerate(((bg2_ref, 0), (bu2_ref, 0), (hidden2_ref, WIDTH))):
+    for kind, at in enumerate((0, 0, WIDTH)):
         cols, rows = pl.ds(at, WIDTH), pl.ds(kind * HALF, HALF)
-        total = mm_first(back_ref[kind], own_ref[:, cols]) + mm_first(lhs_rest[...], rest_ref[:, cols])
+        total = mm(backs[0][kind], own_ref[:, cols]) + mm(backs[1][kind], rest_ref[:, cols])
         out_ref[rows] = total.astype(BF)
         for shift in range(4):
             target = pl.ds(pl.multiple_of(((group + shift) & 3) * 256, 256), 256)
-            copy = pltpu.make_async_copy(out_ref.at[rows, target], out_hbm[shift].at[rows], sems.at[7 + 4 * kind + shift])
+            copy = pltpu.make_async_copy(out_ref.at[rows, target], out_hbm[shift].at[rows], sems.at[5 + 4 * kind + shift])
             stores.append(copy)
             copy.start()
     for store in stores:
         store.wait()
 
 
-def node_body(sel_ref, ret_ref, out_ref):
+def node_body(slot_ref, ret_ref, out_ref, sel_ref):
+    for part in range(3):
+        fill(slot_ref[16 * part : 16 * part + 16].astype(F32), sel_ref, part)
     out_ref[:, :WIDTH] = mm_first(sel_ref[:, :MSG], ret_ref[...]).astype(BF)
     out_ref[:, WIDTH:] = (
         mm_first(sel_ref[:, MSG : 2 * MSG], ret_ref[:, :MID])
@@ -256,7 +257,7 @@
     message, row_sel = call(
         route_body,
         [HBM] * 4,
-        [((MSG, META + 128), VMEM), ((3, MSG, TOKS), HBM)],
+        [((MSG, META + 128), HBM), ((3, MSG, TOKS), HBM)],
         80_000_000,
         1_300_000,
         expert_ids.T,
@@ -268,28 +269,28 @@
             pltpu.VMEM((4, TOKS), BF),
             pltpu.VMEM((TOKS, WIDTH), BF),
             pltpu.VMEM((TOKS, WIDTH), BF),
+            pltpu.VMEM((MSG, META + 128), BF),
             pltpu.VMEM((3, MSG, TOKS), BF),
-            pltpu.SemaphoreType.DMA((5,)),
+            pltpu.SemaphoreType.DMA((8,)),
         ],
     )
     message, *sent = lax.optimization_barrier((message, *own))
     arrived, *rest = lax.optimization_barrier((over_nodes(message), *(other_core(w) for w in sent)))
-    placed, slot_sel = call(
+    placed, node_slots = call(
         place_body,
         [VMEM],
-        [((SENT, 2 * WIDTH), VMEM), ((SENT, 3 * MSG), HBM)],
+        [((SENT, 2 * WIDTH), VMEM), ((48, MSG), VMEM)],
         400_000_000,
         2_300_000,
         arrived,
-        scratch=[pltpu.VMEM((SENT, 3 * MSG), BF), pltpu.VMEM((SENT, 3 * MSG), BF), pltpu.SemaphoreType.DMA],
+        scratch=[pltpu.VMEM((SENT, 3 * MSG), BF)] * 2,
         limit=16,
     )
     rows_own = over_chips(placed)
-    rows_rest = other_core(rows_own)
-    piece, back_own = call(
+    (piece,) = call(
         own_body,
         [VMEM] * 7,
-        [((SENT, WIDTH), VMEM), ((3, SENT, HALF), VMEM)],
+        [((SENT, WIDTH), VMEM)],
         2_300_000_000,
         7_000_000,
         rows_own,
@@ -297,29 +298,38 @@
         *rest,
         limit=24,
     )
+    piece, rows_sent = lax.optimization_barrier((piece, rows_own))
+    rows_rest = other_core(rows_sent)
     returned = over_chips(piece)
     grads = call(
         grads_body,
-        [HBM] * 6,
+        [HBM] * 5,
         [((3 * HALF, 256), HBM)] * 4,
-        2_100_000_000,
+        2_800_000_000,
         8_000_000,
+        rows_own,
+        *own,
         rows_rest,
-        *own,
-        rows_own,
-        back_own,
         scratch=[
             pltpu.VMEM((SENT, 2 * WIDTH), BF),
             *[pltpu.VMEM((HALF, WIDTH), BF)] * 3,
             pltpu.VMEM((SENT, 2 * WIDTH), BF),
-            pltpu.VMEM((3, SENT, HALF), BF),
             pltpu.VMEM((3 * HALF, WIDTH), BF),
-            *[pltpu.VMEM((SENT, HALF), BF)] * 3,
-            pltpu.SemaphoreType.DMA((19,)),
+            pltpu.SemaphoreType.DMA((17,)),
         ],
     )
     returned, *grads = lax.optimization_barrier((returned, *grads))
-    (node_sum,) = call(node_body, [VMEM] * 2, [((MSG, WIDE), VMEM)], 50_000_000_000, 1_300_000, slot_sel, returned, limit=16)
+    (node_sum,) = call(
+        node_body,
+        [VMEM] * 2,
+        [((MSG, WIDE), VMEM)],
+        50_000_000_000,
+        1_300_000,
+        node_slots,
+        returned,
+        scratch=[pltpu.VMEM((SENT, 3 * MSG), BF)],
+        limit=16,
+    )
     (partial,) = call(
         early_body,
         [VMEM] * 2,
@@ -329,6 +339,7 @@
         grads[0],
         *(next_group(grads[shift], shift) for shift in (2,)),
         dtype=F32,
+        limit=24,
     )
     totals = call(
         late_body,
@@ -338,6 +349,7 @@
         2_700_000,
         partial,
         *(next_group(grads[shift], shift) for shift in (1, 3)),
+        limit=24,
     )
     (token_grads,) = call(
         final_body,

time: 144 us -> 142 us (0.986)
  Pallas kernels: 24 us -> 19.5 us
  waiting for transfers between devices: 48.1 us -> 52 us
  local copies, waits for them, and re-layouts: 4.27 us -> 1.8 us
    pallas_call x8, Pallas kernels: 24 us -> 19.5 us  [call(): pl.pallas_call(body, out_shape=tuple((jax.ShapeDtypeStruct(s, dtype) for...]
    ppermute x3, waiting for transfers between devices: 11.1 us -> 14.1 us  [next_group(): return lax.ppermute(x, 'dp', [(i, (i + shift) % 4) for i in range(4)])]
    unnamed x38 -> x28, local copies, waits for them, and re-layouts: 4.27 us -> 1.8 us
    all_to_all x2, waiting for transfers between devices: 31 us -> 32.7 us  [over_nodes(): return lax.all_to_all(x, 'node', split_axis=0, concat_axis=0, tiled=True)]
  transfers between devices with their start and end apart: 10 -> 10, of which waited for: 5 -> 6; matrix products, arithmetic and copies ran while one was open for 0% -> 0% of each run, Pallas kernels for 13% -> 7%
where the time goes in v4:
time: 142 us; the launch traced here: 140 us
  waiting for transfers between devices  52 us (37%)
  starting transfers between devices  48.8 us (34%)
  Pallas kernels  19.5 us (14%)
  blocking collectives  17 us (12%)
  local copies, waits for them, and re-layouts  1.8 us (1%)
    all_to_all x2, waiting for transfers between devices, over_nodes(): return lax.all_to_all(x, 'node', split_axis=0, concat_axis=0, tiled=True)  32.7 us
    all_to_all x2, starting transfers between devices, over_nodes(): return lax.all_to_all(x, 'node', split_axis=0, concat_axis=0, tiled=True)  28 us
    pallas_call x8, Pallas kernels, call(): pl.pallas_call(body, out_shape=tuple((jax.ShapeDtypeStruct(s, dtype) for...  19.5 us
    all_to_all x1, blocking collectives, over_chips(): lax.all_to_all(x, 'local', split_axis=0, concat_axis=0, tiled=True, axis_...  17 us
    ppermute x3, waiting for transfers between devices, next_group(): return lax.ppermute(x, 'dp', [(i, (i + shift) % 4) for i in range(4)])  14.1 us
    ppermute x3, starting transfers between devices, next_group(): return lax.ppermute(x, 'dp', [(i, (i + shift) % 4) for i in range(4)])  9.14 us
    ppermute x4, starting transfers between devices, other_core(): return lax.ppermute(x, 'local', OTHER_CORE)  8.16 us
    all_to_all x1, waiting for transfers between devices, over_chips(): lax.all_to_all(x, 'local', split_axis=0, concat_axis=0, tiled=True, axis_...  3.8 us
  transfers between devices with their start and end apart: 10, of which 6 were waited for; matrix products, arithmetic and copies ran while one was open for 0% of the time, Pallas kernels for 7%

profile of v4, /device:TPU:24, one launch (start us, length us, event | category | flops | bytes accessed | tf_op | source)
XLA Modules:
  0.0 140.1 jit_solution(10984584125463112560)
XLA Ops:
  0.6 0.0 copy-start.3
  0.6 0.0 copy-start.2
  0.7 2.6 %route_body.1 = (bf16[128,3200]{1,0:T(8,128)(2,1)}, bf16[3,128,64]{2,1,0:T(8,128)(2,1)}) custom-call(s32[4,64]{1,0:T(4,128)} %bitcast.36, bf16[4,64]{1,0:T(4,128)(2,1)} %bitcast.37, bf16[64,1024]{1,0:T(8,128)(2,1)} %tok_hbm.1, bf16[64,1024]{1,0:T(8,128)(2,1)} %up_hbm.1), custom_call_target="tpu_custom_call" | custom-call | flops 80000000 | bytes 1300000 | tf_op jit(solution)/shard_map/route_body/pallas_call | solution.py:227
  3.3 15.2 %all-to-all-start = ((bf16[16,8,3200]{2,1,0:T(8,128)(2,1)}), bf16[16,8,3200]{2,1,0:T(8,128)(2,1)S(1)}, u32[]{:S(2)}, u32[]{:S(2)}) async-start(bf16[16,8,3200]{2,1,0:T(8,128)(2,1)} %bitcast.32), calls=%async_computation | async-start | bytes 1638400 | tf_op jit(solution)/shard_map/all_to_all | solution.py:240
  18.5 1.9 %collective-permute-start = (bf16[352,1024]{1,0:T(8,128)(2,1)S(1)}, bf16[352,1024]{1,0:T(8,128)(2,1)S(1)}, u32[]{:S(2)}, u32[]{:S(2)}) collective-permute-start(bf16[352,1024]{1,0:T(8,128)(2,1)S(1)} %bitcast.24), channel_id=1, source_target_pairs={{0,1},{1,0},{2,3},{3,2},{4,5},{5,4},{6,7},{7,6},{8,9},{9,8},{10,11... | collective-permute-start | bytes 2162696 | tf_op jit(solution)/shard_map/ppermute | solution.py:252
  20.5 2.4 %collective-permute-start.1 = (bf16[352,1024]{1,0:T(8,128)(2,1)S(1)}, bf16[352,1024]{1,0:T(8,128)(2,1)S(1)}, u32[]{:S(2)}, u32[]{:S(2)}) collective-permute-start(bf16[352,1024]{1,0:T(8,128)(2,1)S(1)} %bitcast.27), channel_id=1, source_target_pairs={{0,1},{1,0},{2,3},{3,2},{4,5},{5,4},{6,7},{7,6},{8,9},{9,8},{10,11... | collective-permute-start | bytes 2162696 | tf_op jit(solution)/shard_map/ppermute | solution.py:252
  22.9 1.9 %collective-permute-start.2 = (bf16[352,1024]{1,0:T(8,128)(2,1)}, bf16[352,1024]{1,0:T(8,128)(2,1)S(1)}, u32[]{:S(2)}, u32[]{:S(2)}) collective-permute-start(bf16[352,1024]{1,0:T(8,128)(2,1)} %bitcast.29), channel_id=1, source_target_pairs={{0,1},{1,0},{2,3},{3,2},{4,5},{5,4},{6,7},{7,6},{8,9},{9,8},{10,11... | collective-permute-start | bytes 2162696 | tf_op jit(solution)/shard_map/ppermute | solution.py:252
  24.8 0.0 collective-permute-done.refs_3_
  24.8 0.9 copy-done.7
  25.7 1.4 %collective-permute-done.2.refs_5_ = bf16[352,1024]{1,0:T(8,128)(2,1)S(1)} collective-permute-done((bf16[352,1024]{1,0:T(8,128)(2,1)}, bf16[352,1024]{1,0:T(8,128)(2,1)S(1)}, u32[]{:S(2)}, u32[]{:S(2)}) %collective-permute-start.2) | collective-permute-done | bytes 720928 | tf_op jit(solution)/shard_map/ppermute | solution.py:252
  27.2 0.9 copy-done.9
  28.0 31.0 %all-to-all-done = bf16[16,8,3200]{2,1,0:T(8,128)(2,1)S(1)} async-done(((bf16[16,8,3200]{2,1,0:T(8,128)(2,1)}), bf16[16,8,3200]{2,1,0:T(8,128)(2,1)S(1)}, u32[]{:S(2)}, u32[]{:S(2)}) %all-to-all-start) | async-done | bytes 819232 | tf_op jit(solution)/shard_map/all_to_all | solution.py:240
  59.0 1.2 place_body.1
  60.2 0.0 copy-start.4
  60.2 17.0 %all_to_all.46 = bf16[4,80,2048]{2,1,0:T(8,128)(2,1)S(1)} all-to-all(bf16[4,80,2048]{2,1,0:T(8,128)(2,1)S(1)} %bitcast.20), channel_id=1, replica_groups={{0,2,4,6},{1,3,5,7},{8,10,12,14},{9,11,13,15},{16,18,20,22},{17,19,21,2..., dimensions={0} | all-to-all | bytes 2621440 | tf_op jit(solution)/shard_map/all_to_all | solution.py:244
  77.3 4.6 %own_body.1 = bf16[320,1024]{1,0:T(8,128)(2,1)} custom-call(bf16[320,2048]{1,0:T(8,128)(2,1)S(1)} %bitcast.17, bf16[352,1024]{1,0:T(8,128)(2,1)S(1)} %bitcast.25, bf16[352,1024]{1,0:T(8,128)(2,1)S(1)} %bitcast.28, bf16[352,1024]{1,0:T(8,128)(2,1)S(1)} %bitcast.31, bf16[352,1024]{1,0:T(8,128)(2,1)S(1)} %copy-done.6, bf16[352,1024]{1,0:T(8,128)(2,1)S(1)} %copy-done.8, ...), custom_call_target="tpu_custom_call" | custom-call | flops 2300000000 | bytes 7000000 | tf_op jit(solution)/shard_map/own_body/pallas_call | solution.py:227
  81.9 1.9 %collective-permute-start.3 = (bf16[320,2048]{1,0:T(8,128)(2,1)S(1)}, bf16[320,2048]{1,0:T(8,128)(2,1)}, u32[]{:S(2)}, u32[]{:S(2)}) collective-permute-start(bf16[320,2048]{1,0:T(8,128)(2,1)S(1)} %bitcast.18), channel_id=1, source_target_pairs={{0,1},{1,0},{2,3},{3,2},{4,5},{5,4},{6,7},{7,6},{8,9},{9,8},{10,11... | collective-permute-start | bytes 3932168 | tf_op jit(solution)/shard_map/ppermute | solution.py:252
  83.8 3.5 %all-to-all-start.2 = ((bf16[4,80,1024]{2,1,0:T(8,128)(2,1)}), bf16[4,80,1024]{2,1,0:T(8,128)(2,1)S(1)}, u32[]{:S(2)}, u32[]{:S(2)}) async-start(bf16[4,80,1024]{2,1,0:T(8,128)(2,1)} %bitcast.9), calls=%async_computation.2 | async-start | bytes 1310720 | tf_op jit(solution)/shard_map/all_to_all | solution.py:244
  87.3 8.0 %grads_body.1 = (bf16[1056,256]{1,0:T(8,128)(2,1)}, bf16[1056,256]{1,0:T(8,128)(2,1)}, bf16[1056,256]{1,0:T(8,128)(2,1)}, bf16[1056,256]{1,0:T(8,128)(2,1)}) custom-call(bf16[320,2048]{1,0:T(8,128)(2,1)} %bitcast.19, bf16[352,1024]{1,0:T(8,128)(2,1)} %bitcast.23, bf16[352,1024]{1,0:T(8,128)(2,1)} %bitcast.26, bf16[352,1024]{1,0:T(8,128)(2,1)} %bitcast.30, ...), custom_call_target="tpu_custom_call" | custom-call | flops 2800000000 | bytes 8000000 | tf_op jit(solution)/shard_map/grads_body/pallas_call | solution.py:227
  95.3 3.8 %all-to-all-done.2 = bf16[4,80,1024]{2,1,0:T(8,128)(2,1)S(1)} async-done(((bf16[4,80,1024]{2,1,0:T(8,128)(2,1)}), bf16[4,80,1024]{2,1,0:T(8,128)(2,1)S(1)}, u32[]{:S(2)}, u32[]{:S(2)}) %all-to-all-start.2) | async-done | bytes 655392 | tf_op jit(solution)/shard_map/all_to_all | solution.py:244
  99.1 3.1 %collective-permute-start.4 = (bf16[1056,256]{1,0:T(8,128)(2,1)}, bf16[1056,256]{1,0:T(8,128)(2,1)S(1)}, u32[]{:S(2)}, u32[]{:S(2)}) collective-permute-start(bf16[1056,256]{1,0:T(8,128)(2,1)} %get-tuple-element.50), channel_id=1, source_target_pairs={{0,256},{128,384},{256,0},{384,128},{1,257},{129,385},{257,1},{385... | collective-permute-start | bytes 1622024 | tf_op jit(solution)/shard_map/ppermute | solution.py:248
  102.2 1.3 node_body.1
  103.5 12.8 %all-to-all-start.3 = ((bf16[16,8,1536]{2,1,0:T(8,128)(2,1)}), bf16[16,8,1536]{2,1,0:T(8,128)(2,1)S(1)}, u32[]{:S(2)}, u32[]{:S(2)}) async-start(bf16[16,8,1536]{2,1,0:T(8,128)(2,1)} %bitcast.11), calls=%async_computation.3 | async-start | bytes 786432 | tf_op jit(solution)/shard_map/all_to_all | solution.py:240
  116.3 4.1 %collective-permute-start.5 = (bf16[1056,256]{1,0:T(8,128)(2,1)S(1)}, bf16[1056,256]{1,0:T(8,128)(2,1)S(1)}, u32[]{:S(2)}, u32[]{:S(2)}) collective-permute-start(bf16[1056,256]{1,0:T(8,128)(2,1)S(1)} %copy-done.13), channel_id=1, source_target_pairs={{0,128},{128,256},{256,384},{384,0},{1,129},{129,257},{257,385},{3... | collective-permute-start | bytes 1622024 | tf_op jit(solution)/shard_map/ppermute | solution.py:248
  120.4 1.9 %collective-permute-start.6 = (bf16[1056,256]{1,0:T(8,128)(2,1)S(1)}, bf16[1056,256]{1,0:T(8,128)(2,1)S(1)}, u32[]{:S(2)}, u32[]{:S(2)}) collective-permute-start(bf16[1056,256]{1,0:T(8,128)(2,1)S(1)} %copy-done.12), channel_id=1, source_target_pairs={{0,384},{128,0},{256,128},{384,256},{1,385},{129,1},{257,129},{385... | collective-permute-start | bytes 1622024 | tf_op jit(solution)/shard_map/ppermute | solution.py:248
  122.4 0.1 early_body.1.total_ref
  122.5 0.0 copy-start.1
  122.5 9.0 %collective-permute-done.5.refs_0_ = bf16[1056,256]{1,0:T(8,128)(2,1)S(1)} collective-permute-done((bf16[1056,256]{1,0:T(8,128)(2,1)S(1)}, bf16[1056,256]{1,0:T(8,128)(2,1)S(1)}, u32[]{:S(2)}, u32[]{:S(2)}) %collective-permute-start.5) | collective-permute-done | bytes 540704 | tf_op jit(solution)/shard_map/ppermute | solution.py:248
  131.5 5.0 %collective-permute-done.6.refs_1_ = bf16[1056,256]{1,0:T(8,128)(2,1)S(1)} collective-permute-done((bf16[1056,256]{1,0:T(8,128)(2,1)S(1)}, bf16[1056,256]{1,0:T(8,128)(2,1)S(1)}, u32[]{:S(2)}, u32[]{:S(2)}) %collective-permute-start.6) | collective-permute-done | bytes 540704 | tf_op jit(solution)/shard_map/ppermute | solution.py:248
  136.6 0.9 late_body.1
  137.5 1.7 %all-to-all-done.3 = bf16[16,8,1536]{2,1,0:T(8,128)(2,1)S(1)} async-done(((bf16[16,8,1536]{2,1,0:T(8,128)(2,1)}), bf16[16,8,1536]{2,1,0:T(8,128)(2,1)S(1)}, u32[]{:S(2)}, u32[]{:S(2)}) %all-to-all-start.3) | async-done | bytes 393248 | tf_op jit(solution)/shard_map/all_to_all | solution.py:240
  139.1 0.9 final_body.1
  (25 shorter events, 0.1 us)
Async XLA Ops:
  0.6 19.8 %copy-start.3 = (bf16[1,352,1024]{2,1,0:T(8,128)(2,1)S(1)}, bf16[1,352,1024]{2,1,0:T(8,128)(2,1)}, u32[]{:S(2)}) copy-start(bf16[1,352,1024]{2,1,0:T(8,128)(2,1)} %param.12) | copy-start | bytes 2162692
  0.6 17.9 %copy-start.2 = (bf16[1,352,1024]{2,1,0:T(8,128)(2,1)S(1)}, bf16[1,352,1024]{2,1,0:T(8,128)(2,1)}, u32[]{:S(2)}) copy-start(bf16[1,352,1024]{2,1,0:T(8,128)(2,1)} %param.11) | copy-start | bytes 2162692
  3.3 55.7 %all-to-all-start = ((bf16[16,8,3200]{2,1,0:T(8,128)(2,1)}), bf16[16,8,3200]{2,1,0:T(8,128)(2,1)S(1)}, u32[]{:S(2)}, u32[]{:S(2)}) async-start(bf16[16,8,3200]{2,1,0:T(8,128)(2,1)} %bitcast.32), calls=%async_computation | async-start | bytes 1638400 | tf_op jit(solution)/shard_map/all_to_all | solution.py:240
  18.5 6.3 %collective-permute-start = (bf16[352,1024]{1,0:T(8,128)(2,1)S(1)}, bf16[352,1024]{1,0:T(8,128)(2,1)S(1)}, u32[]{:S(2)}, u32[]{:S(2)}) collective-permute-start(bf16[352,1024]{1,0:T(8,128)(2,1)S(1)} %bitcast.24), channel_id=1, source_target_pairs={{0,1},{1,0},{2,3},{3,2},{4,5},{5,4},{6,7},{7,6},{8,9},{9,8},{10,11... | collective-permute-start | bytes 2162696 | tf_op jit(solution)/shard_map/ppermute | solution.py:252
  20.5 4.4 %collective-permute-start.1 = (bf16[352,1024]{1,0:T(8,128)(2,1)S(1)}, bf16[352,1024]{1,0:T(8,128)(2,1)S(1)}, u32[]{:S(2)}, u32[]{:S(2)}) collective-permute-start(bf16[352,1024]{1,0:T(8,128)(2,1)S(1)} %bitcast.27), channel_id=1, source_target_pairs={{0,1},{1,0},{2,3},{3,2},{4,5},{5,4},{6,7},{7,6},{8,9},{9,8},{10,11... | collective-permute-start | bytes 2162696 | tf_op jit(solution)/shard_map/ppermute | solution.py:252
  22.9 4.3 %collective-permute-start.2 = (bf16[352,1024]{1,0:T(8,128)(2,1)}, bf16[352,1024]{1,0:T(8,128)(2,1)S(1)}, u32[]{:S(2)}, u32[]{:S(2)}) collective-permute-start(bf16[352,1024]{1,0:T(8,128)(2,1)} %bitcast.29), channel_id=1, source_target_pairs={{0,1},{1,0},{2,3},{3,2},{4,5},{5,4},{6,7},{7,6},{8,9},{9,8},{10,11... | collective-permute-start | bytes 2162696 | tf_op jit(solution)/shard_map/ppermute | solution.py:252
  24.8 35.4 %copy-start.5 = (bf16[352,1024]{1,0:T(8,128)(2,1)}, bf16[352,1024]{1,0:T(8,128)(2,1)S(1)}, u32[]{:S(2)}) copy-start(bf16[352,1024]{1,0:T(8,128)(2,1)S(1)} %collective-permute-done.refs_3_) | copy-start | bytes 2162692
  24.8 0.9 copy-start.7
  27.2 0.9 copy-start.9
  59.0 18.3 %copy-start.10 = (bf16[352,1024]{1,0:T(8,128)(2,1)S(1)}, bf16[352,1024]{1,0:T(8,128)(2,1)}, u32[]{:S(2)}) copy-start(bf16[352,1024]{1,0:T(8,128)(2,1)} %copy-done.9) | copy-start | bytes 2162692
  60.2 17.1 %copy-start.4 = (bf16[1,352,1024]{2,1,0:T(8,128)(2,1)S(1)}, bf16[1,352,1024]{2,1,0:T(8,128)(2,1)}, u32[]{:S(2)}) copy-start(bf16[1,352,1024]{2,1,0:T(8,128)(2,1)} %param.13) | copy-start | bytes 2162692
  60.2 17.1 %copy-start.6 = (bf16[352,1024]{1,0:T(8,128)(2,1)S(1)}, bf16[352,1024]{1,0:T(8,128)(2,1)}, u32[]{:S(2)}) copy-start(bf16[352,1024]{1,0:T(8,128)(2,1)} %copy-done.5) | copy-start | bytes 2162692
  60.2 17.1 %copy-start.8 = (bf16[352,1024]{1,0:T(8,128)(2,1)S(1)}, bf16[352,1024]{1,0:T(8,128)(2,1)}, u32[]{:S(2)}) copy-start(bf16[352,1024]{1,0:T(8,128)(2,1)} %copy-done.7) | copy-start | bytes 2162692
  77.3 4.6 %copy-start = (bf16[4,80,2048]{2,1,0:T(8,128)(2,1)}, bf16[4,80,2048]{2,1,0:T(8,128)(2,1)S(1)}, u32[]{:S(2)}) copy-start(bf16[4,80,2048]{2,1,0:T(8,128)(2,1)S(1)} %all_to_all.46) | copy-start | bytes 3932164
  81.9 5.4 %collective-permute-start.3 = (bf16[320,2048]{1,0:T(8,128)(2,1)S(1)}, bf16[320,2048]{1,0:T(8,128)(2,1)}, u32[]{:S(2)}, u32[]{:S(2)}) collective-permute-start(bf16[320,2048]{1,0:T(8,128)(2,1)S(1)} %bitcast.18), channel_id=1, source_target_pairs={{0,1},{1,0},{2,3},{3,2},{4,5},{5,4},{6,7},{7,6},{8,9},{9,8},{10,11... | collective-permute-start | bytes 3932168 | tf_op jit(solution)/shard_map/ppermute | solution.py:252
  83.8 15.3 %all-to-all-start.2 = ((bf16[4,80,1024]{2,1,0:T(8,128)(2,1)}), bf16[4,80,1024]{2,1,0:T(8,128)(2,1)S(1)}, u32[]{:S(2)}, u32[]{:S(2)}) async-start(bf16[4,80,1024]{2,1,0:T(8,128)(2,1)} %bitcast.9), calls=%async_computation.2 | async-start | bytes 1310720 | tf_op jit(solution)/shard_map/all_to_all | solution.py:244
  99.1 23.3 %collective-permute-start.4 = (bf16[1056,256]{1,0:T(8,128)(2,1)}, bf16[1056,256]{1,0:T(8,128)(2,1)S(1)}, u32[]{:S(2)}, u32[]{:S(2)}) collective-permute-start(bf16[1056,256]{1,0:T(8,128)(2,1)} %get-tuple-element.50), channel_id=1, source_target_pairs={{0,256},{128,384},{256,0},{384,128},{1,257},{129,385},{257,1},{385... | collective-permute-start | bytes 1622024 | tf_op jit(solution)/shard_map/ppermute | solution.py:248
  102.2 14.1 %copy-start.13 = (bf16[1056,256]{1,0:T(8,128)(2,1)S(1)}, bf16[1056,256]{1,0:T(8,128)(2,1)}, u32[]{:S(2)}) copy-start(bf16[1056,256]{1,0:T(8,128)(2,1)} %get-tuple-element.51) | copy-start | bytes 1622020
  102.2 18.2 %copy-start.12 = (bf16[1056,256]{1,0:T(8,128)(2,1)S(1)}, bf16[1056,256]{1,0:T(8,128)(2,1)}, u32[]{:S(2)}) copy-start(bf16[1056,256]{1,0:T(8,128)(2,1)} %get-tuple-element.52) | copy-start | bytes 1622020
  102.2 20.1 %copy-start.11 = (bf16[1056,256]{1,0:T(8,128)(2,1)S(1)}, bf16[1056,256]{1,0:T(8,128)(2,1)}, u32[]{:S(2)}) copy-start(bf16[1056,256]{1,0:T(8,128)(2,1)} %get-tuple-element.49.refs_0_) | copy-start | bytes 1622020
  103.5 35.7 %all-to-all-start.3 = ((bf16[16,8,1536]{2,1,0:T(8,128)(2,1)}), bf16[16,8,1536]{2,1,0:T(8,128)(2,1)S(1)}, u32[]{:S(2)}, u32[]{:S(2)}) async-start(bf16[16,8,1536]{2,1,0:T(8,128)(2,1)} %bitcast.11), calls=%async_computation.3 | async-start | bytes 786432 | tf_op jit(solution)/shard_map/all_to_all | solution.py:240
  116.3 15.2 %collective-permute-start.5 = (bf16[1056,256]{1,0:T(8,128)(2,1)S(1)}, bf16[1056,256]{1,0:T(8,128)(2,1)S(1)}, u32[]{:S(2)}, u32[]{:S(2)}) collective-permute-start(bf16[1056,256]{1,0:T(8,128)(2,1)S(1)} %copy-done.13), channel_id=1, source_target_pairs={{0,128},{128,256},{256,384},{384,0},{1,129},{129,257},{257,385},{3... | collective-permute-start | bytes 1622024 | tf_op jit(solution)/shard_map/ppermute | solution.py:248
  120.4 16.2 %collective-permute-start.6 = (bf16[1056,256]{1,0:T(8,128)(2,1)S(1)}, bf16[1056,256]{1,0:T(8,128)(2,1)S(1)}, u32[]{:S(2)}, u32[]{:S(2)}) collective-permute-start(bf16[1056,256]{1,0:T(8,128)(2,1)S(1)} %copy-done.12), channel_id=1, source_target_pairs={{0,384},{128,0},{256,128},{384,256},{1,385},{129,1},{257,129},{385... | collective-permute-start | bytes 1622024 | tf_op jit(solution)/shard_map/ppermute | solution.py:248
  122.5 16.6 %copy-start.1 = (bf16[3,128,64]{2,1,0:T(8,128)(2,1)S(1)}, bf16[3,128,64]{2,1,0:T(8,128)(2,1)}, u32[]{:S(2)}) copy-start(bf16[3,128,64]{2,1,0:T(8,128)(2,1)} %get-tuple-element.30.sel_ref) | copy-start | bytes 147460

commit v5 on v4

--- a/solution.py
+++ b/solution.py
@@ -158,22 +158,32 @@
     hbm, out_hbm, vmem, (out_ref, sems) = refs[0:5], refs[5:9], refs[9:14], refs[14:]
     group = lax.axis_index("dp")
     own_ref, gate_ref, up_ref, down_ref, rest_ref = vmem
-    loads = [pltpu.make_async_copy(src, dst, sems.at[i]) for i, (src, dst) in enumerate(zip(hbm, vmem))]
-    for load in loads[:4]:
+    halves = (pl.ds(0, WIDTH), pl.ds(WIDTH, WIDTH))
+    weights = [pltpu.make_async_copy(hbm[i], vmem[i], sems.at[i]) for i in (1, 2, 3)]
+    own_in, rest_in = [
+        [pltpu.make_async_copy(hbm[i].at[:, cols], vmem[i].at[:, cols], sems.at[at + k]) for k, cols in enumerate(halves)]
+        for i, at in ((0, 17), (4, 19))
+    ]
+    for load in (own_in[0], weights[0], weights[1]):
         load.start()
-    for load in loads[:3]:
-        load.wait()
-    loads[4].start()
     backs = []
-    for rows_ref, ready in ((own_ref, loads[3]), (rest_ref, loads[4])):
-        if rows_ref is rest_ref:
-            ready.wait()
+    for rows_ref, loads in ((own_ref, own_in), (rest_ref, rest_in)):
+        first = rows_ref is own_ref
+        loads[0].wait()
+        if first:
+            weights[0].wait()
+            for load in (own_in[1], weights[2], *rest_in):
+                load.start()
         x = rows_ref[:, :WIDTH]
-        gate_logit, up_value = mm_last(gate_ref[...], x), mm_last(up_ref[...], x)
+        gate_logit = mm_last(gate_ref[...], x)
+        if first:
+            weights[1].wait()
+        up_value = mm_last(up_ref[...], x)
         sig = jax.nn.sigmoid(gate_logit)
         act = gate_logit * sig
-        if rows_ref is own_ref:
-            ready.wait()
+        loads[1].wait()
+        if first:
+            weights[2].wait()
         back_hidden = mm_last(down_ref[...], rows_ref[:, WIDTH:])
         slope = up_value * sig * (1.0 + gate_logit * (1.0 - sig))
         backs.append([(back_hidden * slope).astype(BF), (back_hidden * act).astype(BF), (act * up_value).astype(BF)])
@@ -298,8 +308,7 @@
         *rest,
         limit=24,
     )
-    piece, rows_sent = lax.optimization_barrier((piece, rows_own))
-    rows_rest = other_core(rows_sent)
+    rows_rest = other_core(rows_own)
     returned = over_chips(piece)
     grads = call(
         grads_body,
@@ -315,7 +324,7 @@
             *[pltpu.VMEM((HALF, WIDTH), BF)] * 3,
             pltpu.VMEM((SENT, 2 * WIDTH), BF),
             pltpu.VMEM((3 * HALF, WIDTH), BF),
-            pltpu.SemaphoreType.DMA((17,)),
+            pltpu.SemaphoreType.DMA((21,)),
         ],
     )
     returned, *grads = lax.optimization_barrier((returned, *grads))

time: 142 us -> 142 us (level)
  transfers between devices with their start and end apart: 10 -> 10, of which waited for: 6 -> 6; matrix products, arithmetic and copies ran while one was open for 0% -> 0% of each run, Pallas kernels for 7% -> 11%
where the time goes in v5:
time: 142 us; the launch traced here: 140 us
  waiting for transfers between devices  51.7 us (36%)
  starting transfers between devices  48.8 us (34%)
  Pallas kernels  19.7 us (14%)
  blocking collectives  17 us (12%)
  local copies, waits for them, and re-layouts  1.83 us (1%)
    all_to_all x2, waiting for transfers between devices, over_nodes(): return lax.all_to_all(x, 'node', split_axis=0, concat_axis=0, tiled=True)  32.6 us
    all_to_all x2, starting transfers between devices, over_nodes(): return lax.all_to_all(x, 'node', split_axis=0, concat_axis=0, tiled=True)  28 us
    pallas_call x8, Pallas kernels, call(): pl.pallas_call(body, out_shape=tuple((jax.ShapeDtypeStruct(s, dtype) for...  19.7 us
    all_to_all x1, blocking collectives, over_chips(): lax.all_to_all(x, 'local', split_axis=0, concat_axis=0, tiled=True, axis_...  17 us
    ppermute x3, waiting for transfers between devices, next_group(): return lax.ppermute(x, 'dp', [(i, (i + shift) % 4) for i in range(4)])  14.1 us
    ppermute x3, starting transfers between devices, next_group(): return lax.ppermute(x, 'dp', [(i, (i + shift) % 4) for i in range(4)])  9.15 us
    ppermute x4, starting transfers between devices, other_core(): return lax.ppermute(x, 'local', OTHER_CORE)  8.16 us
    all_to_all x1, waiting for transfers between devices, over_chips(): lax.all_to_all(x, 'local', split_axis=0, concat_axis=0, tiled=True, axis_...  3.59 us
  transfers between devices with their start and end apart: 10, of which 6 were waited for; matrix products, arithmetic and copies ran while one was open for 0% of the time, Pallas kernels for 11%

profile of v5, /device:TPU:24, one launch (start us, length us, event | category | flops | bytes accessed | tf_op | source)
XLA Modules:
  0.0 140.0 jit_solution(16812248230390262500)
XLA Ops:
  0.6 0.0 copy-start.3
  0.6 0.0 copy-start.2
  0.7 2.6 %route_body.1 = (bf16[128,3200]{1,0:T(8,128)(2,1)}, bf16[3,128,64]{2,1,0:T(8,128)(2,1)}) custom-call(s32[4,64]{1,0:T(4,128)} %bitcast.36, bf16[4,64]{1,0:T(4,128)(2,1)} %bitcast.37, bf16[64,1024]{1,0:T(8,128)(2,1)} %tok_hbm.1, bf16[64,1024]{1,0:T(8,128)(2,1)} %up_hbm.1), custom_call_target="tpu_custom_call" | custom-call | flops 80000000 | bytes 1300000 | tf_op jit(solution)/shard_map/route_body/pallas_call | solution.py:237
  3.3 15.2 %all-to-all-start = ((bf16[16,8,3200]{2,1,0:T(8,128)(2,1)}), bf16[16,8,3200]{2,1,0:T(8,128)(2,1)S(1)}, u32[]{:S(2)}, u32[]{:S(2)}) async-start(bf16[16,8,3200]{2,1,0:T(8,128)(2,1)} %bitcast.32), calls=%async_computation | async-start | bytes 1638400 | tf_op jit(solution)/shard_map/all_to_all | solution.py:250
  18.5 1.9 %collective-permute-start = (bf16[352,1024]{1,0:T(8,128)(2,1)S(1)}, bf16[352,1024]{1,0:T(8,128)(2,1)S(1)}, u32[]{:S(2)}, u32[]{:S(2)}) collective-permute-start(bf16[352,1024]{1,0:T(8,128)(2,1)S(1)} %bitcast.24), channel_id=1, source_target_pairs={{0,1},{1,0},{2,3},{3,2},{4,5},{5,4},{6,7},{7,6},{8,9},{9,8},{10,11... | collective-permute-start | bytes 2162696 | tf_op jit(solution)/shard_map/ppermute | solution.py:262
  20.5 2.4 %collective-permute-start.1 = (bf16[352,1024]{1,0:T(8,128)(2,1)S(1)}, bf16[352,1024]{1,0:T(8,128)(2,1)S(1)}, u32[]{:S(2)}, u32[]{:S(2)}) collective-permute-start(bf16[352,1024]{1,0:T(8,128)(2,1)S(1)} %bitcast.27), channel_id=1, source_target_pairs={{0,1},{1,0},{2,3},{3,2},{4,5},{5,4},{6,7},{7,6},{8,9},{9,8},{10,11... | collective-permute-start | bytes 2162696 | tf_op jit(solution)/shard_map/ppermute | solution.py:262
  22.9 1.9 %collective-permute-start.2 = (bf16[352,1024]{1,0:T(8,128)(2,1)}, bf16[352,1024]{1,0:T(8,128)(2,1)S(1)}, u32[]{:S(2)}, u32[]{:S(2)}) collective-permute-start(bf16[352,1024]{1,0:T(8,128)(2,1)} %bitcast.29), channel_id=1, source_target_pairs={{0,1},{1,0},{2,3},{3,2},{4,5},{5,4},{6,7},{7,6},{8,9},{9,8},{10,11... | collective-permute-start | bytes 2162696 | tf_op jit(solution)/shard_map/ppermute | solution.py:262
  24.8 0.0 collective-permute-done.refs_3_
  24.8 0.9 copy-done.7
  25.7 1.4 %collective-permute-done.2.refs_5_ = bf16[352,1024]{1,0:T(8,128)(2,1)S(1)} collective-permute-done((bf16[352,1024]{1,0:T(8,128)(2,1)}, bf16[352,1024]{1,0:T(8,128)(2,1)S(1)}, u32[]{:S(2)}, u32[]{:S(2)}) %collective-permute-start.2) | collective-permute-done | bytes 720928 | tf_op jit(solution)/shard_map/ppermute | solution.py:262
  27.2 0.9 copy-done.9
  28.0 31.0 %all-to-all-done = bf16[16,8,3200]{2,1,0:T(8,128)(2,1)S(1)} async-done(((bf16[16,8,3200]{2,1,0:T(8,128)(2,1)}), bf16[16,8,3200]{2,1,0:T(8,128)(2,1)S(1)}, u32[]{:S(2)}, u32[]{:S(2)}) %all-to-all-start) | async-done | bytes 819232 | tf_op jit(solution)/shard_map/all_to_all | solution.py:250
  59.0 1.2 place_body.1
  60.2 0.0 copy-start.4
  60.2 17.0 %all_to_all.46 = bf16[4,80,2048]{2,1,0:T(8,128)(2,1)S(1)} all-to-all(bf16[4,80,2048]{2,1,0:T(8,128)(2,1)S(1)} %bitcast.20), channel_id=1, replica_groups={{0,2,4,6},{1,3,5,7},{8,10,12,14},{9,11,13,15},{16,18,20,22},{17,19,21,2..., dimensions={0} | all-to-all | bytes 2621440 | tf_op jit(solution)/shard_map/all_to_all | solution.py:254
  77.3 1.9 %collective-permute-start.3 = (bf16[320,2048]{1,0:T(8,128)(2,1)S(1)}, bf16[320,2048]{1,0:T(8,128)(2,1)}, u32[]{:S(2)}, u32[]{:S(2)}) collective-permute-start(bf16[320,2048]{1,0:T(8,128)(2,1)S(1)} %bitcast.17), channel_id=1, source_target_pairs={{0,1},{1,0},{2,3},{3,2},{4,5},{5,4},{6,7},{7,6},{8,9},{9,8},{10,11... | collective-permute-start | bytes 3932168 | tf_op jit(solution)/shard_map/ppermute | solution.py:262
  79.2 4.6 %own_body.1 = bf16[320,1024]{1,0:T(8,128)(2,1)} custom-call(bf16[320,2048]{1,0:T(8,128)(2,1)S(1)} %bitcast.18, bf16[352,1024]{1,0:T(8,128)(2,1)S(1)} %bitcast.25, bf16[352,1024]{1,0:T(8,128)(2,1)S(1)} %bitcast.28, bf16[352,1024]{1,0:T(8,128)(2,1)S(1)} %bitcast.31, bf16[352,1024]{1,0:T(8,128)(2,1)S(1)} %copy-done.6, bf16[352,1024]{1,0:T(8,128)(2,1)S(1)} %copy-done.8, ...), custom_call_target="tpu_custom_call" | custom-call | flops 2300000000 | bytes 7000000 | tf_op jit(solution)/shard_map/own_body/pallas_call | solution.py:237
  83.8 3.5 %all-to-all-start.2 = ((bf16[4,80,1024]{2,1,0:T(8,128)(2,1)}), bf16[4,80,1024]{2,1,0:T(8,128)(2,1)S(1)}, u32[]{:S(2)}, u32[]{:S(2)}) async-start(bf16[4,80,1024]{2,1,0:T(8,128)(2,1)} %bitcast.9), calls=%async_computation.2 | async-start | bytes 1310720 | tf_op jit(solution)/shard_map/all_to_all | solution.py:254
  87.3 8.2 %grads_body.1 = (bf16[1056,256]{1,0:T(8,128)(2,1)}, bf16[1056,256]{1,0:T(8,128)(2,1)}, bf16[1056,256]{1,0:T(8,128)(2,1)}, bf16[1056,256]{1,0:T(8,128)(2,1)}) custom-call(bf16[320,2048]{1,0:T(8,128)(2,1)} %bitcast.19, bf16[352,1024]{1,0:T(8,128)(2,1)} %bitcast.23, bf16[352,1024]{1,0:T(8,128)(2,1)} %bitcast.26, bf16[352,1024]{1,0:T(8,128)(2,1)} %bitcast.30, ...), custom_call_target="tpu_custom_call" | custom-call | flops 2800000000 | bytes 8000000 | tf_op jit(solution)/shard_map/grads_body/pallas_call | solution.py:237
  95.5 3.6 %all-to-all-done.2 = bf16[4,80,1024]{2,1,0:T(8,128)(2,1)S(1)} async-done(((bf16[4,80,1024]{2,1,0:T(8,128)(2,1)}), bf16[4,80,1024]{2,1,0:T(8,128)(2,1)S(1)}, u32[]{:S(2)}, u32[]{:S(2)}) %all-to-all-start.2) | async-done | bytes 655392 | tf_op jit(solution)/shard_map/all_to_all | solution.py:254
  99.1 3.1 %collective-permute-start.4 = (bf16[1056,256]{1,0:T(8,128)(2,1)}, bf16[1056,256]{1,0:T(8,128)(2,1)S(1)}, u32[]{:S(2)}, u32[]{:S(2)}) collective-permute-start(bf16[1056,256]{1,0:T(8,128)(2,1)} %get-tuple-element.46), channel_id=1, source_target_pairs={{0,256},{128,384},{256,0},{384,128},{1,257},{129,385},{257,1},{385... | collective-permute-start | bytes 1622024 | tf_op jit(solution)/shard_map/ppermute | solution.py:258
  102.2 1.3 node_body.1
  103.5 12.8 %all-to-all-start.3 = ((bf16[16,8,1536]{2,1,0:T(8,128)(2,1)}), bf16[16,8,1536]{2,1,0:T(8,128)(2,1)S(1)}, u32[]{:S(2)}, u32[]{:S(2)}) async-start(bf16[16,8,1536]{2,1,0:T(8,128)(2,1)} %bitcast.11), calls=%async_computation.3 | async-start | bytes 786432 | tf_op jit(solution)/shard_map/all_to_all | solution.py:250
  116.3 4.1 %collective-permute-start.5 = (bf16[1056,256]{1,0:T(8,128)(2,1)S(1)}, bf16[1056,256]{1,0:T(8,128)(2,1)S(1)}, u32[]{:S(2)}, u32[]{:S(2)}) collective-permute-start(bf16[1056,256]{1,0:T(8,128)(2,1)S(1)} %copy-done.13), channel_id=1, source_target_pairs={{0,128},{128,256},{256,384},{384,0},{1,129},{129,257},{257,385},{3... | collective-permute-start | bytes 1622024 | tf_op jit(solution)/shard_map/ppermute | solution.py:258
  120.4 1.9 %collective-permute-start.6 = (bf16[1056,256]{1,0:T(8,128)(2,1)S(1)}, bf16[1056,256]{1,0:T(8,128)(2,1)S(1)}, u32[]{:S(2)}, u32[]{:S(2)}) collective-permute-start(bf16[1056,256]{1,0:T(8,128)(2,1)S(1)} %copy-done.12), channel_id=1, source_target_pairs={{0,384},{128,0},{256,128},{384,256},{1,385},{129,1},{257,129},{385... | collective-permute-start | bytes 1622024 | tf_op jit(solution)/shard_map/ppermute | solution.py:258
  122.4 0.1 early_body.1.total_ref
  122.5 0.0 copy-start.1
  122.5 9.0 %collective-permute-done.5.refs_0_ = bf16[1056,256]{1,0:T(8,128)(2,1)S(1)} collective-permute-done((bf16[1056,256]{1,0:T(8,128)(2,1)S(1)}, bf16[1056,256]{1,0:T(8,128)(2,1)S(1)}, u32[]{:S(2)}, u32[]{:S(2)}) %collective-permute-start.5) | collective-permute-done | bytes 540704 | tf_op jit(solution)/shard_map/ppermute | solution.py:258
  131.5 5.1 %collective-permute-done.6.refs_1_ = bf16[1056,256]{1,0:T(8,128)(2,1)S(1)} collective-permute-done((bf16[1056,256]{1,0:T(8,128)(2,1)S(1)}, bf16[1056,256]{1,0:T(8,128)(2,1)S(1)}, u32[]{:S(2)}, u32[]{:S(2)}) %collective-permute-start.6) | collective-permute-done | bytes 540704 | tf_op jit(solution)/shard_map/ppermute | solution.py:258
  136.6 0.9 late_body.1
  137.5 1.7 %all-to-all-done.3 = bf16[16,8,1536]{2,1,0:T(8,128)(2,1)S(1)} async-done(((bf16[16,8,1536]{2,1,0:T(8,128)(2,1)}), bf16[16,8,1536]{2,1,0:T(8,128)(2,1)S(1)}, u32[]{:S(2)}, u32[]{:S(2)}) %all-to-all-start.3) | async-done | bytes 393248 | tf_op jit(solution)/shard_map/all_to_all | solution.py:250
  139.1 0.9 final_body.1
  (25 shorter events, 0.1 us)
Async XLA Ops:
  0.6 19.8 %copy-start.3 = (bf16[1,352,1024]{2,1,0:T(8,128)(2,1)S(1)}, bf16[1,352,1024]{2,1,0:T(8,128)(2,1)}, u32[]{:S(2)}) copy-start(bf16[1,352,1024]{2,1,0:T(8,128)(2,1)} %param.12) | copy-start | bytes 2162692
  0.6 17.9 %copy-start.2 = (bf16[1,352,1024]{2,1,0:T(8,128)(2,1)S(1)}, bf16[1,352,1024]{2,1,0:T(8,128)(2,1)}, u32[]{:S(2)}) copy-start(bf16[1,352,1024]{2,1,0:T(8,128)(2,1)} %param.11) | copy-start | bytes 2162692
  3.3 55.7 %all-to-all-start = ((bf16[16,8,3200]{2,1,0:T(8,128)(2,1)}), bf16[16,8,3200]{2,1,0:T(8,128)(2,1)S(1)}, u32[]{:S(2)}, u32[]{:S(2)}) async-start(bf16[16,8,3200]{2,1,0:T(8,128)(2,1)} %bitcast.32), calls=%async_computation | async-start | bytes 1638400 | tf_op jit(solution)/shard_map/all_to_all | solution.py:250
  18.5 6.3 %collective-permute-start = (bf16[352,1024]{1,0:T(8,128)(2,1)S(1)}, bf16[352,1024]{1,0:T(8,128)(2,1)S(1)}, u32[]{:S(2)}, u32[]{:S(2)}) collective-permute-start(bf16[352,1024]{1,0:T(8,128)(2,1)S(1)} %bitcast.24), channel_id=1, source_target_pairs={{0,1},{1,0},{2,3},{3,2},{4,5},{5,4},{6,7},{7,6},{8,9},{9,8},{10,11... | collective-permute-start | bytes 2162696 | tf_op jit(solution)/shard_map/ppermute | solution.py:262
  20.5 4.4 %collective-permute-start.1 = (bf16[352,1024]{1,0:T(8,128)(2,1)S(1)}, bf16[352,1024]{1,0:T(8,128)(2,1)S(1)}, u32[]{:S(2)}, u32[]{:S(2)}) collective-permute-start(bf16[352,1024]{1,0:T(8,128)(2,1)S(1)} %bitcast.27), channel_id=1, source_target_pairs={{0,1},{1,0},{2,3},{3,2},{4,5},{5,4},{6,7},{7,6},{8,9},{9,8},{10,11... | collective-permute-start | bytes 2162696 | tf_op jit(solution)/shard_map/ppermute | solution.py:262
  22.9 4.3 %collective-permute-start.2 = (bf16[352,1024]{1,0:T(8,128)(2,1)}, bf16[352,1024]{1,0:T(8,128)(2,1)S(1)}, u32[]{:S(2)}, u32[]{:S(2)}) collective-permute-start(bf16[352,1024]{1,0:T(8,128)(2,1)} %bitcast.29), channel_id=1, source_target_pairs={{0,1},{1,0},{2,3},{3,2},{4,5},{5,4},{6,7},{7,6},{8,9},{9,8},{10,11... | collective-permute-start | bytes 2162696 | tf_op jit(solution)/shard_map/ppermute | solution.py:262
  24.8 35.4 %copy-start.5 = (bf16[352,1024]{1,0:T(8,128)(2,1)}, bf16[352,1024]{1,0:T(8,128)(2,1)S(1)}, u32[]{:S(2)}) copy-start(bf16[352,1024]{1,0:T(8,128)(2,1)S(1)} %collective-permute-done.refs_3_) | copy-start | bytes 2162692
  24.8 0.9 copy-start.7
  27.2 0.9 copy-start.9
  59.0 20.2 %copy-start.10 = (bf16[352,1024]{1,0:T(8,128)(2,1)S(1)}, bf16[352,1024]{1,0:T(8,128)(2,1)}, u32[]{:S(2)}) copy-start(bf16[352,1024]{1,0:T(8,128)(2,1)} %copy-done.9) | copy-start | bytes 2162692
  60.2 19.0 %copy-start.4 = (bf16[1,352,1024]{2,1,0:T(8,128)(2,1)S(1)}, bf16[1,352,1024]{2,1,0:T(8,128)(2,1)}, u32[]{:S(2)}) copy-start(bf16[1,352,1024]{2,1,0:T(8,128)(2,1)} %param.13) | copy-start | bytes 2162692
  60.2 19.0 %copy-start.6 = (bf16[352,1024]{1,0:T(8,128)(2,1)S(1)}, bf16[352,1024]{1,0:T(8,128)(2,1)}, u32[]{:S(2)}) copy-start(bf16[352,1024]{1,0:T(8,128)(2,1)} %copy-done.5) | copy-start | bytes 2162692
  60.2 19.0 %copy-start.8 = (bf16[352,1024]{1,0:T(8,128)(2,1)S(1)}, bf16[352,1024]{1,0:T(8,128)(2,1)}, u32[]{:S(2)}) copy-start(bf16[352,1024]{1,0:T(8,128)(2,1)} %copy-done.7) | copy-start | bytes 2162692
  77.3 6.5 %copy-start = (bf16[4,80,2048]{2,1,0:T(8,128)(2,1)}, bf16[4,80,2048]{2,1,0:T(8,128)(2,1)S(1)}, u32[]{:S(2)}) copy-start(bf16[4,80,2048]{2,1,0:T(8,128)(2,1)S(1)} %all_to_all.46) | copy-start | bytes 3932164
  77.3 10.0 %collective-permute-start.3 = (bf16[320,2048]{1,0:T(8,128)(2,1)S(1)}, bf16[320,2048]{1,0:T(8,128)(2,1)}, u32[]{:S(2)}, u32[]{:S(2)}) collective-permute-start(bf16[320,2048]{1,0:T(8,128)(2,1)S(1)} %bitcast.17), channel_id=1, source_target_pairs={{0,1},{1,0},{2,3},{3,2},{4,5},{5,4},{6,7},{7,6},{8,9},{9,8},{10,11... | collective-permute-start | bytes 3932168 | tf_op jit(solution)/shard_map/ppermute | solution.py:262
  83.8 15.3 %all-to-all-start.2 = ((bf16[4,80,1024]{2,1,0:T(8,128)(2,1)}), bf16[4,80,1024]{2,1,0:T(8,128)(2,1)S(1)}, u32[]{:S(2)}, u32[]{:S(2)}) async-start(bf16[4,80,1024]{2,1,0:T(8,128)(2,1)} %bitcast.9), calls=%async_computation.2 | async-start | bytes 1310720 | tf_op jit(solution)/shard_map/all_to_all | solution.py:254
  99.1 23.3 %collective-permute-start.4 = (bf16[1056,256]{1,0:T(8,128)(2,1)}, bf16[1056,256]{1,0:T(8,128)(2,1)S(1)}, u32[]{:S(2)}, u32[]{:S(2)}) collective-permute-start(bf16[1056,256]{1,0:T(8,128)(2,1)} %get-tuple-element.46), channel_id=1, source_target_pairs={{0,256},{128,384},{256,0},{384,128},{1,257},{129,385},{257,1},{385... | collective-permute-start | bytes 1622024 | tf_op jit(solution)/shard_map/ppermute | solution.py:258
  102.2 14.1 %copy-start.13 = (bf16[1056,256]{1,0:T(8,128)(2,1)S(1)}, bf16[1056,256]{1,0:T(8,128)(2,1)}, u32[]{:S(2)}) copy-start(bf16[1056,256]{1,0:T(8,128)(2,1)} %get-tuple-element.47) | copy-start | bytes 1622020
  102.2 18.2 %copy-start.12 = (bf16[1056,256]{1,0:T(8,128)(2,1)S(1)}, bf16[1056,256]{1,0:T(8,128)(2,1)}, u32[]{:S(2)}) copy-start(bf16[1056,256]{1,0:T(8,128)(2,1)} %get-tuple-element.48) | copy-start | bytes 1622020
  102.2 20.1 %copy-start.11 = (bf16[1056,256]{1,0:T(8,128)(2,1)S(1)}, bf16[1056,256]{1,0:T(8,128)(2,1)}, u32[]{:S(2)}) copy-start(bf16[1056,256]{1,0:T(8,128)(2,1)} %get-tuple-element.45.refs_0_) | copy-start | bytes 1622020
  103.5 35.6 %all-to-all-start.3 = ((bf16[16,8,1536]{2,1,0:T(8,128)(2,1)}), bf16[16,8,1536]{2,1,0:T(8,128)(2,1)S(1)}, u32[]{:S(2)}, u32[]{:S(2)}) async-start(bf16[16,8,1536]{2,1,0:T(8,128)(2,1)} %bitcast.11), calls=%async_computation.3 | async-start | bytes 786432 | tf_op jit(solution)/shard_map/all_to_all | solution.py:250
  116.3 15.2 %collective-permute-start.5 = (bf16[1056,256]{1,0:T(8,128)(2,1)S(1)}, bf16[1056,256]{1,0:T(8,128)(2,1)S(1)}, u32[]{:S(2)}, u32[]{:S(2)}) collective-permute-start(bf16[1056,256]{1,0:T(8,128)(2,1)S(1)} %copy-done.13), channel_id=1, source_target_pairs={{0,128},{128,256},{256,384},{384,0},{1,129},{129,257},{257,385},{3... | collective-permute-start | bytes 1622024 | tf_op jit(solution)/shard_map/ppermute | solution.py:258
  120.4 16.2 %collective-permute-start.6 = (bf16[1056,256]{1,0:T(8,128)(2,1)S(1)}, bf16[1056,256]{1,0:T(8,128)(2,1)S(1)}, u32[]{:S(2)}, u32[]{:S(2)}) collective-permute-start(bf16[1056,256]{1,0:T(8,128)(2,1)S(1)} %copy-done.12), channel_id=1, source_target_pairs={{0,384},{128,0},{256,128},{384,256},{1,385},{129,1},{257,129},{385... | collective-permute-start | bytes 1622024 | tf_op jit(solution)/shard_map/ppermute | solution.py:258
  122.5 16.6 %copy-start.1 = (bf16[3,128,64]{2,1,0:T(8,128)(2,1)S(1)}, bf16[3,128,64]{2,1,0:T(8,128)(2,1)}, u32[]{:S(2)}) copy-start(bf16[3,128,64]{2,1,0:T(8,128)(2,1)} %get-tuple-element.28.sel_ref) | copy-start | bytes 147460
